TPU v7x, 256 devices: a whole 4x4x8 slice. The times are simulated.
256 devices in a mesh: xy: 64 (over y_lo, x, z), gz: 4 (over y_hi, core).
Axes of the slice: x: 4, y: 4 (y_hi: 2, y_lo: 2; y = y_hi * 2 + y_lo), z: 8, core: 2. Of those that a mesh axis runs over, the one named last changes fastest.
Arguments:
- velocity: float32 [3, 256, 128, 512], P(None, 'xy', 'gz'), may hold values from -6 to 6
- pressure: float32 [256, 128, 512], P('xy', 'gz'), may hold values from -6 to 6
- momentum_source: float32 [3, 256, 128, 512], P(None, 'xy', 'gz'), may hold values from -6 to 6
- continuity_source: float32 [256, 128, 512], P('xy', 'gz'), may hold values from -6 to 6
- reaction: float32 [256, 128, 512], P('xy', 'gz'), may hold values from 0.01 to 0.2
- pressure_weight: float32 [256, 512], P('xy'), may hold values from 0.5 to 2
- mz_inverse: float32 [128, 128], replicated, as said below
Outputs:
- velocity_update: float32 [3, 256, 128, 512], P(None, 'xy', 'gz')
- correction: float32 [256, 128, 512], P('xy', 'gz')
Inputs may be any that keep to these rules, and one draw needn't show every extreme that they name: mz_inverse is a full 128 x 128 matrix.
All inputs are finite; a program needn't handle non-finite values.
Results may differ from a plain program's by a relative error of at most 0.00007.
Values sent between devices are 32-bit elements; how exact they have to be, the bound alone decides.
A program may use at most 64 MiB of HBM per device.

v0:
```python
import jax
import jax.numpy as jnp
from jax import lax
from jax.sharding import PartitionSpec as P

MASS_TAPS = (
    1.0 / 5040.0,
    1.0 / 42.0,
    397.0 / 1680.0,
    151.0 / 315.0,
    397.0 / 1680.0,
    1.0 / 42.0,
    1.0 / 5040.0,
)
STIFF_TAPS = (-1.0 / 120.0, -0.2, -0.125, 2.0 / 3.0, -0.125, -0.2, -1.0 / 120.0)
DAMPING = 0.5
CENTRE_DIAG = 3.0 * (2.0 / 3.0) * (151.0 / 315.0) ** 2


def extended(cells, sides, width):
    for axis, dim in sides:
        count = lax.axis_size(axis)
        ends = count - 1
        head = lax.slice_in_dim(cells, 0, width, axis=dim)
        tail = lax.slice_in_dim(cells, cells.shape[dim] - width, cells.shape[dim], axis=dim)
        cells = jnp.concatenate(
            [
                lax.ppermute(tail, axis, [(i, (i + 1) % count) for i in range(ends)]),
                cells,
                lax.ppermute(head, axis, [((i + 1) % count, i) for i in range(ends)]),
            ],
            axis=dim,
        )
    return cells


def shifted_2(value, axis, steps):
    count = lax.axis_size(axis)
    initial, last = (max(0, -steps), min(count, count - steps))
    return lax.ppermute(value, axis, [(source, source + steps) for source in range(initial, last)])


def apply_band(values, weights, direction):
    length = values.shape[direction] - 6
    summed = weights[0] * lax.slice_in_dim(values, 0, length, axis=direction)
    for offset in range(1, 7):
        summed = summed + weights[offset] * lax.slice_in_dim(
            values, offset, offset + length, axis=direction
        )
    return summed


def widen_last(values):
    return jnp.pad(values, ((0, 0), (0, 0), (0, 0), (3, 3)))


def inner_parts(values):
    mass_z = widen_last(apply_band(values, MASS_TAPS, 2))
    stiff_z = widen_last(apply_band(values, STIFF_TAPS, 2))
    outer_mass = apply_band(mass_z, MASS_TAPS, 3)
    outer_stiff = apply_band(mass_z, STIFF_TAPS, 3) + apply_band(stiff_z, MASS_TAPS, 3)
    return (outer_mass, outer_stiff)


def along_y_part(values):
    shifted = jnp.pad(values[1], ((0, 0), (0, 0), (0, 1)))[:, :, 1:]
    return shifted - values[1]


def operate(values, reaction, with_div):
    rows_x = values.shape[1]
    rows_z = values.shape[2]
    diverged = None
    padded = extended(values, (("xy", 1), ("gz", 2)), 3)
    outer_mass, outer_stiff = inner_parts(padded)
    applied = (
        apply_band(outer_mass, STIFF_TAPS, 1)
        + apply_band(outer_stiff, MASS_TAPS, 1)
        + reaction * values
    )
    if with_div:
        along_x = padded[0, 4 : 4 + rows_x, 3 : 3 + rows_z] - values[0]
        along_z = padded[2, 3 : 3 + rows_x, 4 : 4 + rows_z] - values[2]
        diverged = along_x + along_y_part(values) + along_z
    return (applied, diverged)


def local_gradient(potential, west_plane, lower_plane):
    prev_x = jnp.concatenate([west_plane, potential[:-1]], axis=0)
    prev_z = jnp.concatenate([lower_plane, potential[:, :-1]], axis=1)
    prev_y = jnp.pad(potential, ((0, 0), (0, 0), (1, 0)))[:, :, :-1]
    return jnp.stack([prev_x - potential, prev_y - potential, prev_z - potential])


def shards(
    velocity, pressure, momentum_source, continuity_source, reaction, pressure_weight, mz_inverse
):
    applied, diverged = operate(velocity, reaction, True)
    west_plane = shifted_2(pressure[-1:], "xy", 1)
    lower_plane = shifted_2(pressure[:, -1:], "gz", 1)
    pressure_grad = local_gradient(pressure, west_plane, lower_plane)
    pressure_residual = continuity_source - diverged
    scaled = -pressure_weight[:, None, :] * pressure_residual
    solved = jnp.einsum(
        "zk,xky->xzy",
        mz_inverse,
        lax.all_to_all(scaled, "gz", split_axis=0, concat_axis=1, tiled=True),
        precision=lax.Precision.HIGHEST,
    )
    correction = lax.all_to_all(solved, "gz", split_axis=1, concat_axis=0, tiled=True)
    west_corr = shifted_2(correction[-1:], "xy", 1)
    lower_corr = shifted_2(correction[:, -1:], "gz", 1)
    right_side = (
        momentum_source
        - applied
        - pressure_grad
        - local_gradient(correction, west_corr, lower_corr)
    )
    diagonal = CENTRE_DIAG + reaction
    first_sweep = DAMPING * right_side / diagonal
    applied_sweep, unused_div = operate(first_sweep, reaction, False)
    second_sweep = first_sweep + DAMPING * (right_side - applied_sweep) / diagonal
    return (second_sweep, correction)


def solution(mesh):
    return jax.shard_map(
        shards,
        mesh=mesh,
        in_specs=(
            P(None, "xy", "gz", None),
            P("xy", "gz", None),
            P(None, "xy", "gz", None),
            P("xy", "gz", None),
            P("xy", "gz", None),
            P("xy", None),
            P(),
        ),
        out_specs=(P(None, "xy", "gz", None), P("xy", "gz", None)),
        check_vma=False,
    )
```

profile of v0, /device:TPU:9, one launch (start us, length us, event | category | flops | bytes accessed | tf_op | source)
XLA Modules:
  0.0 158.8 jit_solution(14131879285902479097)
XLA Ops:
  0.6 0.0 copy-start
  0.7 0.0 copy-start.6
  0.7 1.5 fusion.85
  2.2 3.5 %collective-permute-start = (f32[3,3,32,512]{3,2,1,0:T(8,128)S(1)}, f32[3,3,32,512]{3,2,1,0:T(8,128)S(1)}, u32[]{:S(2)}, u32[]{:S(2)}) collective-permute-start(f32[3,3,32,512]{3,2,1,0:T(8,128)S(1)} %get-tuple-element.23), channel_id=1, source_target_pairs={{0,4},{4,8},{8,12},{12,16},{16,20},{20,24},{24,28},{28,32},{32,36}... | collective-permute-start | bytes 1769480 | tf_op jit(solution)/shard_map/ppermute | solution.py:28
  5.7 4.8 %collective-permute-start.5 = (f32[4,1,512]{2,1,0:T(1,128)S(1)}, f32[4,1,512]{2,1,0:T(1,128)S(1)}, u32[]{:S(2)}, u32[]{:S(2)}) collective-permute-start(f32[4,1,512]{2,1,0:T(1,128)S(1)} %slice.352), channel_id=1, source_target_pairs={{0,1},{1,2},{2,3},{4,5},{5,6},{6,7},{8,9},{9,10},{10,11},{12,13},{... | collective-permute-start | bytes 24584 | tf_op jit(solution)/shard_map/ppermute | solution.py:40
  10.5 3.5 %collective-permute-start.4 = (f32[1,32,512]{2,1,0:T(8,128)S(1)}, f32[1,32,512]{2,1,0:T(8,128)S(1)}, u32[]{:S(2)}, u32[]{:S(2)}) collective-permute-start(f32[1,32,512]{2,1,0:T(8,128)S(1)} %slice.349), channel_id=1, source_target_pairs={{0,4},{4,8},{8,12},{12,16},{16,20},{20,24},{24,28},{28,32},{32,36}... | collective-permute-start | bytes 196616 | tf_op jit(solution)/shard_map/ppermute | solution.py:40
  14.1 6.9 %collective-permute-start.1 = (f32[3,3,32,512]{3,2,1,0:T(8,128)S(1)}, f32[3,3,32,512]{3,2,1,0:T(8,128)S(1)}, u32[]{:S(2)}, u32[]{:S(2)}) collective-permute-start(f32[3,3,32,512]{3,2,1,0:T(8,128)S(1)} %get-tuple-element.22), channel_id=1, source_target_pairs={{4,0},{8,4},{12,8},{16,12},{20,16},{24,20},{28,24},{32,28},{36,32}... | collective-permute-start | bytes 1769480 | tf_op jit(solution)/shard_map/ppermute | solution.py:30
  21.1 0.7 broadcast_add_fusion
  21.8 2.9 %collective-permute-done = f32[3,3,32,512]{3,2,1,0:T(8,128)S(1)} collective-permute-done((f32[3,3,32,512]{3,2,1,0:T(8,128)S(1)}, f32[3,3,32,512]{3,2,1,0:T(8,128)S(1)}, u32[]{:S(2)}, u32[]{:S(2)}) %collective-permute-start) | collective-permute-done | bytes 589856 | tf_op jit(solution)/shard_map/ppermute | solution.py:28
  24.8 0.1 constant_dynamic-update-slice_fusion.1
  24.9 0.0 copy-start.14
  24.9 6.7 %collective-permute-done.1 = f32[3,3,32,512]{3,2,1,0:T(8,128)S(1)} collective-permute-done((f32[3,3,32,512]{3,2,1,0:T(8,128)S(1)}, f32[3,3,32,512]{3,2,1,0:T(8,128)S(1)}, u32[]{:S(2)}, u32[]{:S(2)}) %collective-permute-start.1) | collective-permute-done | bytes 589856 | tf_op jit(solution)/shard_map/ppermute | solution.py:30
  31.7 0.8 fusion.83
  32.5 1.9 %collective-permute-start.3 = (f32[3,10,3,512]{3,2,1,0:T(4,128)S(1)}, f32[3,10,3,512]{3,2,1,0:T(4,128)S(1)}, u32[]{:S(2)}, u32[]{:S(2)}) collective-permute-start(f32[3,10,3,512]{3,2,1,0:T(4,128)S(1)} %get-tuple-element.19), channel_id=1, source_target_pairs={{1,0},{2,1},{3,2},{5,4},{6,5},{7,6},{9,8},{10,9},{11,10},{13,12},{... | collective-permute-start | bytes 552968 | tf_op jit(solution)/shard_map/ppermute | solution.py:30
  34.4 1.0 fusion.79
  35.4 5.1 %collective-permute-start.2 = (f32[3,10,3,512]{3,2,1,0:T(4,128)}, f32[3,10,3,512]{3,2,1,0:T(4,128)}, u32[]{:S(2)}, u32[]{:S(2)}) collective-permute-start(f32[3,10,3,512]{3,2,1,0:T(4,128)} %get-tuple-element.18), channel_id=1, source_target_pairs={{0,1},{1,2},{2,3},{4,5},{5,6},{6,7},{8,9},{9,10},{10,11},{12,13},{... | collective-permute-start | bytes 552968 | tf_op jit(solution)/shard_map/ppermute | solution.py:28
  40.6 0.9 collective-permute-done.3
  41.5 0.7 copy-done.12
  42.2 0.9 fusion.72
  43.1 3.4 %all-to-all-start = ((f32[4,32,512]{2,1,0:T(8,128)}), f32[4,32,512]{2,1,0:T(8,128)S(1)}, u32[]{:S(2)}, u32[]{:S(2)}) async-start(f32[4,32,512]{2,1,0:T(8,128)} %fusion.72), calls=%async_computation | async-start | bytes 524288 | tf_op jit(solution)/shard_map/all_to_all | solution.py:107
  46.5 6.6 %multiply_add_fusion.5 = (f32[3,10,32,512]{3,2,1,0:T(8,128)}, f32[3,10,32,512]{3,2,1,0:T(8,128)}) fusion(f32[3,10,32,512]{3,2,1,0:T(8,128)S(1)} %constant_dynamic-update-slice_fusion, f32[3,10,3,512]{3,2,1,0:T(4,128)} %collective-permute-done.2, f32[3,10,3,512]{3,2,1,0:T(4,128)} %copy-done.12), kind=kLoop, calls=%fused_computation.74 | loop fusion | flops 18186240 | bytes 6266880 | tf_op jit(solution)/shard_map/add | solution.py:47
  53.1 0.6 convolution_bitcast_fusion
  53.7 0.8 copy.21
  54.5 4.0 %all-to-all-start.1 = ((f32[1,128,512]{2,0,1:T(1,128)}), f32[1,128,512]{2,0,1:T(1,128)}, u32[]{:S(2)}, u32[]{:S(2)}) async-start(f32[1,128,512]{2,0,1:T(1,128)} %copy.21), calls=%async_computation.1 | async-start | bytes 524288 | tf_op jit(solution)/shard_map/all_to_all | solution.py:110
  58.6 21.0 %multiply_add_fusion.4 = (f32[3,10,32,512]{3,2,1,0:T(8,128)S(1)}, f32[3,10,32,512]{3,2,1,0:T(8,128)}) fusion(f32[3,10,32,512]{3,2,1,0:T(8,128)} %get-tuple-element.8, f32[3,10,32,512]{3,2,1,0:T(8,128)} %get-tuple-element.9), kind=kLoop, calls=%fused_computation.73 | loop fusion | flops 19660800 | bytes 7864320 | tf_op jit(solution)/shard_map/add | solution.py:47
  79.6 1.1 copy.23
  80.8 4.4 %collective-permute-start.7 = (f32[4,1,512]{2,1,0:T(1,128)S(1)}, f32[4,1,512]{2,1,0:T(1,128)S(1)}, u32[]{:S(2)}, u32[]{:S(2)}) collective-permute-start(f32[4,1,512]{2,1,0:T(1,128)S(1)} %slice.430), channel_id=1, source_target_pairs={{0,1},{1,2},{2,3},{4,5},{5,6},{6,7},{8,9},{9,10},{10,11},{12,13},{... | collective-permute-start | bytes 24584 | tf_op jit(solution)/shard_map/ppermute | solution.py:40
  85.3 2.4 %collective-permute-start.6 = (f32[1,32,512]{2,1,0:T(8,128)S(1)}, f32[1,32,512]{2,1,0:T(8,128)S(1)}, u32[]{:S(2)}, u32[]{:S(2)}) collective-permute-start(f32[1,32,512]{2,1,0:T(8,128)S(1)} %slice_bitcast_fusion.2), channel_id=1, source_target_pairs={{0,4},{4,8},{8,12},{12,16},{16,20},{20,24},{24,28},{28,32},{32,36}... | collective-permute-start | bytes 196616 | tf_op jit(solution)/shard_map/ppermute | solution.py:40
  87.7 0.1 fusion.74
  87.8 0.9 slice.429
  88.8 6.1 %collective-permute-done.6 = f32[1,32,512]{2,1,0:T(8,128)S(1)} collective-permute-done((f32[1,32,512]{2,1,0:T(8,128)S(1)}, f32[1,32,512]{2,1,0:T(8,128)S(1)}, u32[]{:S(2)}, u32[]{:S(2)}) %collective-permute-start.6) | collective-permute-done | bytes 65568 | tf_op jit(solution)/shard_map/ppermute | solution.py:40
  94.9 0.1 maximum_subtract_fusion.2
  95.1 2.6 %multiply_divide_fusion = (f32[3,4,32,512]{3,2,1,0:T(8,128)S(1)}, f32[3,4,32,512]{3,2,1,0:T(8,128)}) fusion(f32[4,32,512]{2,1,0:T(8,128)S(1)} %copy-done.8, f32[1,4,32,512]{3,2,1,0:T(8,128)S(1)} %get-tuple-element.28, f32[1,4,32,512]{3,2,1,0:T(8,128)S(1)} %fusion.74, f32[1,4,32,512]{3,2,1,0:T(8,128)S(1)} %get-tuple-element.27, ...), kind=kLoop, calls=%fused_computation.139 | loop fusion | flops 7471104 | bytes 16252928 | tf_op jit(solution)/shard_map/div | solution.py:120
  97.7 0.1 fusion.84
  97.9 1.9 %collective-permute-start.8 = (f32[3,3,32,512]{3,2,1,0:T(8,128)S(1)}, f32[3,3,32,512]{3,2,1,0:T(8,128)S(1)}, u32[]{:S(2)}, u32[]{:S(2)}) collective-permute-start(f32[3,3,32,512]{3,2,1,0:T(8,128)S(1)} %get-tuple-element.20), channel_id=1, source_target_pairs={{0,4},{4,8},{8,12},{12,16},{16,20},{20,24},{24,28},{28,32},{32,36}... | collective-permute-start | bytes 1769480 | tf_op jit(solution)/shard_map/ppermute | solution.py:28
  99.8 7.6 %collective-permute-start.9 = (f32[3,3,32,512]{3,2,1,0:T(8,128)S(1)}, f32[3,3,32,512]{3,2,1,0:T(8,128)S(1)}, u32[]{:S(2)}, u32[]{:S(2)}) collective-permute-start(f32[3,3,32,512]{3,2,1,0:T(8,128)S(1)} %get-tuple-element.21), channel_id=1, source_target_pairs={{4,0},{8,4},{12,8},{16,12},{20,16},{24,20},{28,24},{32,28},{36,32}... | collective-permute-start | bytes 1769480 | tf_op jit(solution)/shard_map/ppermute | solution.py:30
  107.4 11.2 %collective-permute-done.8 = f32[3,3,32,512]{3,2,1,0:T(8,128)S(1)} collective-permute-done((f32[3,3,32,512]{3,2,1,0:T(8,128)S(1)}, f32[3,3,32,512]{3,2,1,0:T(8,128)S(1)}, u32[]{:S(2)}, u32[]{:S(2)}) %collective-permute-start.8) | collective-permute-done | bytes 589856 | tf_op jit(solution)/shard_map/ppermute | solution.py:28
  118.6 1.7 %collective-permute-done.9 = f32[3,3,32,512]{3,2,1,0:T(8,128)S(1)} collective-permute-done((f32[3,3,32,512]{3,2,1,0:T(8,128)S(1)}, f32[3,3,32,512]{3,2,1,0:T(8,128)S(1)}, u32[]{:S(2)}, u32[]{:S(2)}) %collective-permute-start.9) | collective-permute-done | bytes 589856 | tf_op jit(solution)/shard_map/ppermute | solution.py:30
  120.2 0.3 pad_maximum_fusion.2
  120.5 0.1 fusion.82
  120.6 1.9 %collective-permute-start.10 = (f32[3,10,3,512]{3,2,1,0:T(4,128)S(1)}, f32[3,10,3,512]{3,2,1,0:T(4,128)S(1)}, u32[]{:S(2)}, u32[]{:S(2)}) collective-permute-start(f32[3,10,3,512]{3,2,1,0:T(4,128)S(1)} %get-tuple-element.14), channel_id=1, source_target_pairs={{0,1},{1,2},{2,3},{4,5},{5,6},{6,7},{8,9},{9,10},{10,11},{12,13},{... | collective-permute-start | bytes 552968 | tf_op jit(solution)/shard_map/ppermute | solution.py:28
  122.5 2.6 %collective-permute-start.11 = (f32[3,10,3,512]{3,2,1,0:T(4,128)S(1)}, f32[3,10,3,512]{3,2,1,0:T(4,128)S(1)}, u32[]{:S(2)}, u32[]{:S(2)}) collective-permute-start(f32[3,10,3,512]{3,2,1,0:T(4,128)S(1)} %get-tuple-element.15), channel_id=1, source_target_pairs={{1,0},{2,1},{3,2},{5,4},{6,5},{7,6},{9,8},{10,9},{11,10},{13,12},{... | collective-permute-start | bytes 552968 | tf_op jit(solution)/shard_map/ppermute | solution.py:30
  125.1 0.5 collective-permute-done.10
  125.6 5.9 %collective-permute-done.11 = f32[3,10,3,512]{3,2,1,0:T(4,128)S(1)} collective-permute-done((f32[3,10,3,512]{3,2,1,0:T(4,128)S(1)}, f32[3,10,3,512]{3,2,1,0:T(4,128)S(1)}, u32[]{:S(2)}, u32[]{:S(2)}) %collective-permute-start.11) | collective-permute-done | bytes 184352 | tf_op jit(solution)/shard_map/ppermute | solution.py:30
  131.5 0.7 maximum_maximum_fusion
  132.2 3.7 %multiply_add_fusion.2 = (f32[3,10,32,512]{3,2,1,0:T(8,128)}, f32[3,10,32,512]{3,2,1,0:T(8,128)}) fusion(f32[3,10,35,512]{3,2,1,0:T(8,128)S(1)} %get-tuple-element.13, f32[3,10,35,512]{3,2,1,0:T(8,128)S(1)} %get-tuple-element.12, f32[3,3,32,512]{3,2,1,0:T(8,128)S(1)} %collective-permute-done.9, f32[3,4,32,512]{3,2,1,0:T(8,128)S(1)} %get-tuple-element.4, ...), kind=kLoop, calls=%fused_computation.71 | loop fusion | flops 13762560 | bytes 17694720 | tf_op jit(solution)/shard_map/add | solution.py:47
  135.9 20.0 %multiply_add_fusion.1 = (f32[3,10,32,512]{3,2,1,0:T(8,128)S(1)}, f32[3,10,32,512]{3,2,1,0:T(8,128)S(1)}) fusion(f32[3,10,32,512]{3,2,1,0:T(8,128)} %get-tuple-element.6, f32[3,10,32,512]{3,2,1,0:T(8,128)} %get-tuple-element.7), kind=kLoop, calls=%fused_computation.70 | loop fusion | flops 19660800 | bytes 7864320 | tf_op jit(solution)/shard_map/add | solution.py:47
  156.0 2.8 %fusion.37 = f32[3,4,32,512]{3,2,1,0:T(8,128)} fusion(f32[3,4,32,512]{3,2,1,0:T(8,128)S(1)} %copy-done.4, f32[3,10,32,512]{3,2,1,0:T(8,128)S(1)} %get-tuple-element.11, f32[3,10,32,512]{3,2,1,0:T(8,128)S(1)} %get-tuple-element.10, f32[4,32,512]{2,1,0:T(8,128)} %broadcast_add_fusion, f32[4,32,512]{2,1,0:T(8,128)S(1)} %copy-done.7), kind=kLoop, calls=%fused_computation.83 | loop fusion | flops 6881280 | bytes 13107200 | tf_op jit(solution)/shard_map/add | solution.py:122
  (45 shorter events, 0.3 us)
Async XLA Ops:
  0.6 52.4 %copy-start = (f32[128,128]{1,0:T(8,128)S(1)}, f32[128,128]{1,0:T(8,128)}, u32[]{:S(2)}) copy-start(f32[128,128]{1,0:T(8,128)} %param.13) | copy-start | bytes 196612
  0.6 20.4 %copy-start.2 = (f32[3,4,32,512]{3,2,1,0:T(8,128)S(1)}, f32[3,4,32,512]{3,2,1,0:T(8,128)}, u32[]{:S(2)}) copy-start(f32[3,4,32,512]{3,2,1,0:T(8,128)} %param.7) | copy-start | bytes 2359300
  0.7 5.1 %copy-start.5 = (f32[4,32,512]{2,1,0:T(8,128)S(1)}, f32[4,32,512]{2,1,0:T(8,128)}, u32[]{:S(2)}) copy-start(f32[4,32,512]{2,1,0:T(8,128)} %param.8) | copy-start | bytes 786436
  0.7 20.4 %copy-start.15 = (f32[4,512]{1,0:T(4,128)S(1)}, f32[4,512]{1,0:T(4,128)}, u32[]{:S(2)}) copy-start(f32[4,512]{1,0:T(4,128)} %param.12) | copy-start | bytes 24580
  0.7 20.4 %copy-start.6 = (f32[4,32,512]{2,1,0:T(8,128)S(1)}, f32[4,32,512]{2,1,0:T(8,128)}, u32[]{:S(2)}) copy-start(f32[4,32,512]{2,1,0:T(8,128)} %param.11) | copy-start | bytes 786436
  2.2 22.6 %collective-permute-start = (f32[3,3,32,512]{3,2,1,0:T(8,128)S(1)}, f32[3,3,32,512]{3,2,1,0:T(8,128)S(1)}, u32[]{:S(2)}, u32[]{:S(2)}) collective-permute-start(f32[3,3,32,512]{3,2,1,0:T(8,128)S(1)} %get-tuple-element.23), channel_id=1, source_target_pairs={{0,4},{4,8},{8,12},{12,16},{16,20},{20,24},{24,28},{28,32},{32,36}... | collective-permute-start | bytes 1769480 | tf_op jit(solution)/shard_map/ppermute | solution.py:28
  5.7 28.7 %collective-permute-start.5 = (f32[4,1,512]{2,1,0:T(1,128)S(1)}, f32[4,1,512]{2,1,0:T(1,128)S(1)}, u32[]{:S(2)}, u32[]{:S(2)}) collective-permute-start(f32[4,1,512]{2,1,0:T(1,128)S(1)} %slice.352), channel_id=1, source_target_pairs={{0,1},{1,2},{2,3},{4,5},{5,6},{6,7},{8,9},{9,10},{10,11},{12,13},{... | collective-permute-start | bytes 24584 | tf_op jit(solution)/shard_map/ppermute | solution.py:40
  10.5 23.9 %collective-permute-start.4 = (f32[1,32,512]{2,1,0:T(8,128)S(1)}, f32[1,32,512]{2,1,0:T(8,128)S(1)}, u32[]{:S(2)}, u32[]{:S(2)}) collective-permute-start(f32[1,32,512]{2,1,0:T(8,128)S(1)} %slice.349), channel_id=1, source_target_pairs={{0,4},{4,8},{8,12},{12,16},{16,20},{20,24},{24,28},{28,32},{32,36}... | collective-permute-start | bytes 196616 | tf_op jit(solution)/shard_map/ppermute | solution.py:40
  14.1 17.6 %collective-permute-start.1 = (f32[3,3,32,512]{3,2,1,0:T(8,128)S(1)}, f32[3,3,32,512]{3,2,1,0:T(8,128)S(1)}, u32[]{:S(2)}, u32[]{:S(2)}) collective-permute-start(f32[3,3,32,512]{3,2,1,0:T(8,128)S(1)} %get-tuple-element.22), channel_id=1, source_target_pairs={{4,0},{8,4},{12,8},{16,12},{20,16},{24,20},{28,24},{32,28},{36,32}... | collective-permute-start | bytes 1769480 | tf_op jit(solution)/shard_map/ppermute | solution.py:30
  24.9 17.3 %copy-start.14 = (f32[4,32,512]{2,1,0:T(8,128)S(1)}, f32[4,32,512]{2,1,0:T(8,128)}, u32[]{:S(2)}) copy-start(f32[4,32,512]{2,1,0:T(8,128)} %param.10) | copy-start | bytes 786436
  32.5 9.0 %collective-permute-start.3 = (f32[3,10,3,512]{3,2,1,0:T(4,128)S(1)}, f32[3,10,3,512]{3,2,1,0:T(4,128)S(1)}, u32[]{:S(2)}, u32[]{:S(2)}) collective-permute-start(f32[3,10,3,512]{3,2,1,0:T(4,128)S(1)} %get-tuple-element.19), channel_id=1, source_target_pairs={{1,0},{2,1},{3,2},{5,4},{6,5},{7,6},{9,8},{10,9},{11,10},{13,12},{... | collective-permute-start | bytes 552968 | tf_op jit(solution)/shard_map/ppermute | solution.py:30
  35.4 11.1 %collective-permute-start.2 = (f32[3,10,3,512]{3,2,1,0:T(4,128)}, f32[3,10,3,512]{3,2,1,0:T(4,128)}, u32[]{:S(2)}, u32[]{:S(2)}) collective-permute-start(f32[3,10,3,512]{3,2,1,0:T(4,128)} %get-tuple-element.18), channel_id=1, source_target_pairs={{0,1},{1,2},{2,3},{4,5},{5,6},{6,7},{8,9},{9,10},{10,11},{12,13},{... | collective-permute-start | bytes 552968 | tf_op jit(solution)/shard_map/ppermute | solution.py:28
  41.5 0.7 copy-start.12
  43.1 10.0 %all-to-all-start = ((f32[4,32,512]{2,1,0:T(8,128)}), f32[4,32,512]{2,1,0:T(8,128)S(1)}, u32[]{:S(2)}, u32[]{:S(2)}) async-start(f32[4,32,512]{2,1,0:T(8,128)} %fusion.72), calls=%async_computation | async-start | bytes 524288 | tf_op jit(solution)/shard_map/all_to_all | solution.py:107
  54.5 25.0 %all-to-all-start.1 = ((f32[1,128,512]{2,0,1:T(1,128)}), f32[1,128,512]{2,0,1:T(1,128)}, u32[]{:S(2)}, u32[]{:S(2)}) async-start(f32[1,128,512]{2,0,1:T(1,128)} %copy.21), calls=%async_computation.1 | async-start | bytes 524288 | tf_op jit(solution)/shard_map/all_to_all | solution.py:110
  79.5 15.5 %copy-start.1 = (f32[3,10,32,512]{3,2,1,0:T(8,128)S(1)}, f32[3,10,32,512]{3,2,1,0:T(8,128)}, u32[]{:S(2)}) copy-start(f32[3,10,32,512]{3,2,1,0:T(8,128)} %get-tuple-element.17) | copy-start | bytes 5898244
  79.6 15.5 %copy-start.8 = (f32[4,32,512]{2,1,0:T(8,128)S(1)}, f32[4,32,512]{2,1,0:T(8,128)}, u32[]{:S(2)}) copy-start(f32[4,32,512]{2,1,0:T(8,128)} %broadcast_add_fusion) | copy-start | bytes 786436
  79.6 15.5 %copy-start.9 = (f32[1,4,32,512]{3,2,1,0:T(8,128)S(1)}, f32[1,4,32,512]{3,2,1,0:T(8,128)}, u32[]{:S(2)}) copy-start(f32[1,4,32,512]{3,2,1,0:T(8,128)} %get-tuple-element.24) | copy-start | bytes 786436
  79.6 15.5 %copy-start.10 = (f32[1,4,32,512]{3,2,1,0:T(8,128)S(1)}, f32[1,4,32,512]{3,2,1,0:T(8,128)}, u32[]{:S(2)}) copy-start(f32[1,4,32,512]{3,2,1,0:T(8,128)} %get-tuple-element.25) | copy-start | bytes 786436
  79.6 15.5 %copy-start.11 = (f32[1,4,32,512]{3,2,1,0:T(8,128)S(1)}, f32[1,4,32,512]{3,2,1,0:T(8,128)}, u32[]{:S(2)}) copy-start(f32[1,4,32,512]{3,2,1,0:T(8,128)} %get-tuple-element.26) | copy-start | bytes 786436
  79.6 15.5 %copy-start.13 = (f32[3,4,32,512]{3,2,1,0:T(8,128)S(1)}, f32[3,4,32,512]{3,2,1,0:T(8,128)}, u32[]{:S(2)}) copy-start(f32[3,4,32,512]{3,2,1,0:T(8,128)} %param.9) | copy-start | bytes 2359300
  80.7 17.0 %copy-start.3 = (f32[1,128,512]{2,1,0:T(8,128)}, f32[1,128,512]{2,1,0:T(8,128)S(1)}, u32[]{:S(2)}) copy-start(f32[1,128,512]{2,1,0:T(8,128)S(1)} %copy.23) | copy-start | bytes 786436
  80.8 8.0 %collective-permute-start.7 = (f32[4,1,512]{2,1,0:T(1,128)S(1)}, f32[4,1,512]{2,1,0:T(1,128)S(1)}, u32[]{:S(2)}, u32[]{:S(2)}) collective-permute-start(f32[4,1,512]{2,1,0:T(1,128)S(1)} %slice.430), channel_id=1, source_target_pairs={{0,1},{1,2},{2,3},{4,5},{5,6},{6,7},{8,9},{9,10},{10,11},{12,13},{... | collective-permute-start | bytes 24584 | tf_op jit(solution)/shard_map/ppermute | solution.py:40
  85.3 9.7 %collective-permute-start.6 = (f32[1,32,512]{2,1,0:T(8,128)S(1)}, f32[1,32,512]{2,1,0:T(8,128)S(1)}, u32[]{:S(2)}, u32[]{:S(2)}) collective-permute-start(f32[1,32,512]{2,1,0:T(8,128)S(1)} %slice_bitcast_fusion.2), channel_id=1, source_target_pairs={{0,4},{4,8},{8,12},{12,16},{16,20},{20,24},{24,28},{28,32},{32,36}... | collective-permute-start | bytes 196616 | tf_op jit(solution)/shard_map/ppermute | solution.py:40
  97.9 20.7 %collective-permute-start.8 = (f32[3,3,32,512]{3,2,1,0:T(8,128)S(1)}, f32[3,3,32,512]{3,2,1,0:T(8,128)S(1)}, u32[]{:S(2)}, u32[]{:S(2)}) collective-permute-start(f32[3,3,32,512]{3,2,1,0:T(8,128)S(1)} %get-tuple-element.20), channel_id=1, source_target_pairs={{0,4},{4,8},{8,12},{12,16},{16,20},{20,24},{24,28},{28,32},{32,36}... | collective-permute-start | bytes 1769480 | tf_op jit(solution)/shard_map/ppermute | solution.py:28
  99.8 20.4 %collective-permute-start.9 = (f32[3,3,32,512]{3,2,1,0:T(8,128)S(1)}, f32[3,3,32,512]{3,2,1,0:T(8,128)S(1)}, u32[]{:S(2)}, u32[]{:S(2)}) collective-permute-start(f32[3,3,32,512]{3,2,1,0:T(8,128)S(1)} %get-tuple-element.21), channel_id=1, source_target_pairs={{4,0},{8,4},{12,8},{16,12},{20,16},{24,20},{28,24},{32,28},{36,32}... | collective-permute-start | bytes 1769480 | tf_op jit(solution)/shard_map/ppermute | solution.py:30
  120.6 5.0 %collective-permute-start.10 = (f32[3,10,3,512]{3,2,1,0:T(4,128)S(1)}, f32[3,10,3,512]{3,2,1,0:T(4,128)S(1)}, u32[]{:S(2)}, u32[]{:S(2)}) collective-permute-start(f32[3,10,3,512]{3,2,1,0:T(4,128)S(1)} %get-tuple-element.14), channel_id=1, source_target_pairs={{0,1},{1,2},{2,3},{4,5},{5,6},{6,7},{8,9},{9,10},{10,11},{12,13},{... | collective-permute-start | bytes 552968 | tf_op jit(solution)/shard_map/ppermute | solution.py:28
  122.5 9.0 %collective-permute-start.11 = (f32[3,10,3,512]{3,2,1,0:T(4,128)S(1)}, f32[3,10,3,512]{3,2,1,0:T(4,128)S(1)}, u32[]{:S(2)}, u32[]{:S(2)}) collective-permute-start(f32[3,10,3,512]{3,2,1,0:T(4,128)S(1)} %get-tuple-element.15), channel_id=1, source_target_pairs={{1,0},{2,1},{3,2},{5,4},{6,5},{7,6},{9,8},{10,9},{11,10},{13,12},{... | collective-permute-start | bytes 552968 | tf_op jit(solution)/shard_map/ppermute | solution.py:30
  135.9 20.0 %copy-start.4 = (f32[3,4,32,512]{3,2,1,0:T(8,128)S(1)}, f32[3,4,32,512]{3,2,1,0:T(8,128)}, u32[]{:S(2)}) copy-start(f32[3,4,32,512]{3,2,1,0:T(8,128)} %get-tuple-element.5) | copy-start | bytes 2359300
  135.9 20.0 %copy-start.7 = (f32[4,32,512]{2,1,0:T(8,128)S(1)}, f32[4,32,512]{2,1,0:T(8,128)}, u32[]{:S(2)}) copy-start(f32[4,32,512]{2,1,0:T(8,128)} %param.11) | copy-start | bytes 786436
where the time goes:
time: 160 us; the launch traced here: 159 us
  other arithmetic  60.4 us (38%)
  starting transfers between devices  54.2 us (34%)
  waiting for transfers between devices  36 us (22%)
  local copies, waits for them, and re-layouts  6.44 us (4%)
    add x4, other arithmetic, apply_band(): summed + weights[offset] * lax.slice_in_dim(values, offset, offset + leng...  51.3 us
    ppermute x4, starting transfers between devices, extended(): lax.ppermute(head, axis, [((i + 1) % count, i) for i in range(ends)])  19 us
    ppermute x4, waiting for transfers between devices, extended(): lax.ppermute(head, axis, [((i + 1) % count, i) for i in range(ends)])  15.2 us
    ppermute x4, starting transfers between devices, shifted_2(): lax.ppermute(value, axis, [(source, source + steps) for source in range(i...  15.2 us
    ppermute x4, waiting for transfers between devices, extended(): lax.ppermute(tail, axis, [(i, (i + 1) % count) for i in range(ends)])  14.6 us
    ppermute x4, starting transfers between devices, extended(): lax.ppermute(tail, axis, [(i, (i + 1) % count) for i in range(ends)])  12.5 us
    ppermute x4, waiting for transfers between devices, shifted_2(): lax.ppermute(value, axis, [(source, source + steps) for source in range(i...  6.13 us
    all_to_all x1, starting transfers between devices, shards(): lax.all_to_all(solved, 'gz', split_axis=1, concat_axis=0, tiled=True)  4.03 us
  transfers between devices with their start and end apart: 14, of which 8 were waited for; matrix products, arithmetic and copies ran while one was open for 20% of the time, Pallas kernels for 0%

commit v1 on v0

v1 whole, which is shorter than its diff:
```python
import functools

import jax
import jax.numpy as jnp
import ml_dtypes
import numpy as np
from jax import lax
from jax.experimental import pallas as pl
from jax.experimental.pallas import tpu as pltpu
from jax.sharding import PartitionSpec as P

MASS_INT = (1.0, 120.0, 1191.0, 2416.0, 1191.0, 120.0, 1.0)
STIFF_INT = (-1.0, -24.0, -15.0, 80.0, -15.0, -24.0, -1.0)
MASS_SCALE = 5040.0
STIFF_SCALE = 120.0
DAMPING = 0.5
CENTRE_DIAG = 3.0 * (2.0 / 3.0) * (151.0 / 315.0) ** 2

PX = 4
PZ = 32
ROWS = PX * PZ
NY = 512
HALO = 3 * PZ
EDGE = 80
DEPTH = ROWS + 2 * HALO + EDGE
MESH = pl.DeviceIdType.MESH
F32 = jnp.float32
BF16 = jnp.bfloat16


def split_np(matrix):
    high = matrix.astype(ml_dtypes.bfloat16)
    low = (matrix - high.astype(np.float64)).astype(ml_dtypes.bfloat16)
    return high, low


def source_points():
    points = [(p, z) for p in range(PX) for z in range(PZ)]
    points += [(p, z) for p in (-3, -2, -1) for z in range(PZ)]
    points += [(p, z) for p in (4, 5, 6) for z in range(PZ)]
    inner, outer = tuple(range(PX)), (-3, -2, -1, 4, 5, 6)
    for planes in (inner, outer):
        for first in (-4, PZ):
            points += [(p, first + j) for p in planes for j in range(4)]
    return points


def operators():
    mass = {o: w / MASS_SCALE for o, w in zip(range(-3, 4), MASS_INT)}
    stiff = {o: w / STIFF_SCALE for o, w in zip(range(-3, 4), STIFF_INT)}
    plane = np.zeros((2 * ROWS, DEPTH), np.float64)
    for column, (x_in, z_in) in enumerate(source_points()):
        for x_out in range(PX):
            for z_out in range(PZ):
                ox, oz = x_in - x_out, z_in - z_out
                if abs(ox) <= 3 and abs(oz) <= 3:
                    row = x_out * PZ + z_out
                    plane[row, column] = (mass[ox] * stiff[oz] + stiff[ox] * mass[oz]) / MASS_SCALE
                    plane[ROWS + row, column] = mass[ox] * mass[oz] / STIFF_SCALE
    mass_y = np.zeros((NY, NY), np.float64)
    stiff_y = np.zeros((NY, NY), np.float64)
    for offset in range(-3, 4):
        mass_y += np.diag(np.full(NY - abs(offset), MASS_INT[offset + 3]), -offset)
        stiff_y += np.diag(np.full(NY - abs(offset), STIFF_INT[offset + 3]), -offset)
    return split_np(plane) + split_np(mass_y) + split_np(stiff_y)[:1]


def split(values):
    high = values.astype(BF16)
    return high, (values - high.astype(F32)).astype(BF16)


def dot(left, right):
    return jnp.dot(left, right, preferred_element_type=F32)


def kernel(
    count_x,
    vel, prs, mom, con, rea, pwt, mzi, sh_a, sl_a, mh_a, ml_a, ky_a,
    out, cor,
    V, PR, MS, CS, RE, PW, MZ, SH, SL, MH, ML, KY,
    XL, XR, ZB, PK, SG, QH, PD, PP, Q, CO, H, BASE, FS, OB, BH, BL, SBH, SBL, QL,
    local_sem, out_sem, send_sem, recv_sem,
):
    i = lax.axis_index("xy")
    g = lax.axis_index("gz")
    left = (lax.rem(i + count_x - 1, count_x), g)
    right = (lax.rem(i + 1, count_x), g)
    upper = (i, lax.rem(g + 1, 4))
    lower = (i, lax.rem(g + 3, 4))
    across = (i, lax.rem(g + 2, 4))
    core = (i, g + 1 - 2 * lax.rem(g, 2))
    has_left, has_right = i > 0, i < count_x - 1
    has_lower, has_upper = g > 0, g < 3

    loads = []

    def load(src, dst):
        copy = pltpu.make_async_copy(src, dst, local_sem.at[len(loads)])
        copy.start()
        loads.append(copy)
        return copy

    load_v = {c: load(vel.at[c], V.at[c]) for c in (2, 0, 1)}
    load_p = load(prs, PR)
    load_c = load(con, CS)
    load_w = load(pwt, PW)
    load_z = load(mzi.at[pl.ds(pl.multiple_of(g * PZ, PZ), PZ)], MZ.at[pl.ds(8, PZ)])
    load_r = load(rea, RE)
    load_ops = [load(a, b) for a, b in ((sh_a, SH), (sl_a, SL), (mh_a, MH), (ml_a, ML), (ky_a, KY))]
    load_m = load(mom, MS)
    above = pl.multiple_of(jnp.maximum(g * PZ - 8, 0), 8)
    load_z2 = pltpu.make_async_copy(mzi.at[pl.ds(above, 8)], MZ.at[pl.ds(0, 8)], local_sem.at[len(loads)])

    @pl.when(has_lower)
    def _():
        load_z2.start()

    @pl.when(jnp.logical_not(has_left))
    def _():
        XL[...] = jnp.zeros_like(XL)
        QH[...] = jnp.zeros_like(QH)

    @pl.when(jnp.logical_not(has_right))
    def _():
        XR[...] = jnp.zeros_like(XR)

    @pl.when(jnp.logical_not(has_lower))
    def _():
        MZ[0:8, :] = jnp.zeros((8, 128), F32)
        PD[...] = jnp.zeros_like(PD)
        for s in range(2):
            for c in range(3):
                ZB[s, c, 0:16, :] = jnp.zeros((16, NY), F32)
                ZB[s, c, 32:56, :] = jnp.zeros((24, NY), F32)

    @pl.when(jnp.logical_not(has_upper))
    def _():
        for s in range(2):
            for c in range(3):
                ZB[s, c, 16:32, :] = jnp.zeros((16, NY), F32)
                ZB[s, c, 56:80, :] = jnp.zeros((24, NY), F32)

    used = [0]

    def remote(src, dst, device, sends, receives):
        at = used[0]
        used[0] += 1
        copy = pltpu.make_async_remote_copy(
            src_ref=src, dst_ref=dst, send_sem=send_sem.at[at], recv_sem=recv_sem.at[at],
            device_id=device, device_id_type=MESH,
        )
        return copy, sends, receives

    started = []

    def start(*copies):
        condition = copies[0][1]
        started.extend(copies)
        if condition is None:
            for copy in copies:
                copy[0].start()
        else:

            @pl.when(condition)
            def _():
                for copy in copies:
                    copy[0].start()

    def arrive(*copies):
        condition = copies[0][2]
        if condition is None:
            for copy in copies:
                copy[0].wait_recv()
        else:

            @pl.when(condition)
            def _():
                for copy in copies:
                    copy[0].wait_recv()

    def to_left(src, dst):
        return remote(src, dst, left, has_left, has_right)

    def to_right(src, dst):
        return remote(src, dst, right, has_right, has_left)

    def to_upper(src, dst):
        return remote(src, dst, upper, has_upper, has_lower)

    def to_lower(src, dst):
        return remote(src, dst, lower, has_lower, has_upper)

    barrier = pltpu.get_barrier_semaphore()
    for device in (left, right, upper, lower, across):
        pl.semaphore_signal(barrier, inc=1, device_id=device, device_id_type=MESH)
    pl.semaphore_wait(barrier, 5)

    v_left = {c: to_left(vel.at[c, pl.ds(0, HALO)], XR.at[0, c]) for c in (1, 2)}
    v_first = to_left(vel.at[0, pl.ds(0, PZ)], XR.at[0, 0, pl.ds(0, PZ)])
    v_left[0] = to_left(vel.at[0, pl.ds(PZ, 2 * PZ)], XR.at[0, 0, pl.ds(PZ, 2 * PZ)])
    v_right = {c: to_right(vel.at[c, pl.ds(PZ, HALO)], XL.at[0, c]) for c in range(3)}
    start(v_first, v_left[1], v_left[2], v_left[0])
    start(v_right[1], v_right[2], v_right[0])

    def edges(s, c, ref):
        for p in range(PX):
            PK[s, c, pl.ds(4 * p, 4), :] = ref[c, pl.ds(p * PZ + PZ - 4, 4), :]
            PK[s, c, pl.ds(16 + 4 * p, 4), :] = ref[c, pl.ds(p * PZ, 4), :]
        down = to_lower(PK.at[s, c, pl.ds(16, 16)], ZB.at[s, c, pl.ds(16, 16)])
        up = to_upper(PK.at[s, c, pl.ds(0, 16)], ZB.at[s, c, pl.ds(0, 16)])
        start(down)
        start(up)
        return down, up

    def corners(s, c):
        for half, ref in enumerate((XL, XR)):
            for p in range(3):
                at = 12 * half + 4 * p
                PK[s, c, pl.ds(32 + at, 4), :] = ref[s, c, pl.ds(p * PZ + PZ - 4, 4), :]
                PK[s, c, pl.ds(56 + at, 4), :] = ref[s, c, pl.ds(p * PZ, 4), :]
        down = to_lower(PK.at[s, c, pl.ds(56, 24)], ZB.at[s, c, pl.ds(56, 24)])
        up = to_upper(PK.at[s, c, pl.ds(32, 24)], ZB.at[s, c, pl.ds(32, 24)])
        start(down)
        start(up)
        return down, up

    edge, corner = {}, {}
    load_v[2].wait()
    edge[0, 2] = edges(0, 2, V)
    load_p.wait()
    for p in range(PX):
        PP[pl.ds(p, 1), :] = PR[pl.ds(p * PZ + PZ - 1, 1), :]
    PP[pl.ds(4, 4), :] = jnp.zeros((4, NY), F32)
    p_rows = to_upper(PP, PD)
    start(p_rows)
    load_v[0].wait()
    load_v[1].wait()
    edge[0, 1] = edges(0, 1, V)
    edge[0, 0] = edges(0, 0, V)

    row_at = lax.broadcasted_iota(jnp.int32, (PZ, NY), 0)
    lane_at = lax.broadcasted_iota(jnp.int32, (PZ, NY), 1)

    def plane(p):
        return pl.ds(p * PZ, PZ)

    mine = pl.ds(pl.multiple_of(g * PZ, PZ), PZ)
    theirs = pl.ds(pl.multiple_of(lax.rem(g + 2, 4) * PZ, PZ), PZ)
    s_across = [remote(SG.at[p, mine], SG.at[p, mine], across, None, None) for p in range(PX)]
    s_core = [remote(SG.at[p, mine], SG.at[p, mine], core, None, None) for p in range(PX)]
    s_next = [remote(SG.at[p, theirs], SG.at[p, theirs], core, None, None) for p in range(PX)]

    def residual(p):
        vx, vy, vz = (V[c, plane(p), :] for c in range(3))
        next_x = XR[0, 0, pl.ds(0, PZ), :] if p == PX - 1 else V[0, plane(p + 1), :]
        next_y = jnp.where(lane_at == NY - 1, 0.0, pltpu.roll(vy, NY - 1, 1))
        beyond = ZB[0, 2, pl.ds(16 + 4 * p, 1), :]
        next_z = jnp.where(row_at == PZ - 1, beyond, pltpu.roll(vz, PZ - 1, 0))
        diverged = (next_x - vx) + (next_y - vy) + (next_z - vz)
        SG[p, mine, :] = -PW[pl.ds(p, 1), :] * (CS[plane(p), :] - diverged)
        start(s_across[p], s_core[p])

    load_c.wait()
    load_w.wait()
    arrive(edge[0, 2][0])
    for p in range(PX - 1):
        residual(p)
    arrive(v_first)
    residual(PX - 1)

    load_r.wait()
    H[...] = DAMPING / (CENTRE_DIAG + RE[...])
    for copy in load_ops:
        copy.wait()
    load_m.wait()
    load_z.wait()

    @pl.when(has_lower)
    def _():
        load_z2.wait()

    def operate(s, c, ref):
        BH[0:ROWS, :], BL[0:ROWS, :] = split(ref[c])
        BH[ROWS:ROWS + HALO, :], BL[ROWS:ROWS + HALO, :] = split(XL[s, c])
        BH[ROWS + HALO:ROWS + 2 * HALO, :], BL[ROWS + HALO:ROWS + 2 * HALO, :] = split(XR[s, c])
        BH[ROWS + 2 * HALO:, :], BL[ROWS + 2 * HALO:, :] = split(ZB[s, c])
        both = dot(SH[...], BH[...]) + (dot(SL[...], BH[...]) + dot(SH[...], BL[...]))
        first_h, first_l = split(both[:ROWS])
        second_h, second_l = split(both[ROWS:])
        mass, stiff = MH[...], KY[...]
        return (dot(first_h, mass) + dot(second_h, stiff)) + (
            dot(first_l, mass) + dot(second_l, stiff) + dot(first_h, ML[...])
        )

    def base(c):
        BASE[c] = MS[c] - operate(0, c, V) - RE[...] * V[c]

    mz_h, mz_l = split(MZ[...])

    def solve(p):
        s_h, s_l = split(SG[p])
        solved = dot(mz_h, s_h) + (dot(mz_l, s_h) + dot(mz_h, s_l))
        CO[plane(p), :] = solved[8:]
        Q[plane(p), :] = solved[8:] + PR[plane(p), :]
        QL[pl.ds(p, 1), :] = solved[7:8] + PD[pl.ds(p, 1), :]

    arrive(v_left[1])
    arrive(v_right[1])
    corner[0, 1] = corners(0, 1)
    for p in range(PX):
        arrive(s_across[p])
        start(s_next[p])
        if p == 2:
            arrive(edge[0, 1][0], corner[0, 1][0])
            arrive(edge[0, 1][1], corner[0, 1][1])
            base(1)
    arrive(v_left[2])
    arrive(v_right[2])
    corner[0, 2] = corners(0, 2)
    arrive(p_rows)
    for p in range(PX):
        arrive(s_core[p], s_next[p])
        solve(p)
    q_plane = to_right(Q.at[plane(PX - 1)], QH)
    start(q_plane)
    c_out = pltpu.make_async_copy(CO, cor, out_sem.at[3])
    c_out.start()

    f_left, f_right = {}, {}

    def sweep(c):
        for p in range(PX):
            q = Q[plane(p), :]
            if c == 0:
                before = QH[...] if p == 0 else Q[plane(p - 1), :]
            elif c == 1:
                before = jnp.where(lane_at == 0, 0.0, pltpu.roll(q, 1, 1))
            else:
                before = jnp.where(row_at == 0, QL[pl.ds(p, 1), :], pltpu.roll(q, 1, 0))
            FS[c, plane(p), :] = H[plane(p), :] * (BASE[c, plane(p), :] - (before - q))
        f_left[c] = to_left(FS.at[c, pl.ds(0, HALO)], XR.at[1, c])
        f_right[c] = to_right(FS.at[c, pl.ds(PZ, HALO)], XL.at[1, c])
        start(f_left[c])
        start(f_right[c])
        edge[1, c] = edges(1, c, FS)

    sweep(1)
    arrive(edge[0, 2][1], corner[0, 2][1])
    arrive(corner[0, 2][0])
    base(2)
    sweep(2)
    arrive(v_left[0])
    arrive(v_right[0])
    corner[0, 0] = corners(0, 0)
    arrive(edge[0, 0][0], corner[0, 0][0])
    arrive(edge[0, 0][1], corner[0, 0][1])
    base(0)
    arrive(q_plane)
    sweep(0)

    outs = []
    for c in (1, 2, 0):
        arrive(f_left[c])
        arrive(f_right[c])
        corner[1, c] = corners(1, c)
        arrive(edge[1, c][0], corner[1, c][0])
        arrive(edge[1, c][1], corner[1, c][1])
        OB[c] = FS[c] * (2.0 - RE[...] * H[...]) - H[...] * operate(1, c, FS)
        copy = pltpu.make_async_copy(OB.at[c], out.at[c], out_sem.at[c])
        copy.start()
        outs.append(copy)

    for copy, sends, _ in started:
        if sends is None:
            copy.wait_send()
        else:
            pl.when(sends)(copy.wait_send)
    c_out.wait()
    for copy in outs:
        copy.wait()


def shards(count_x, velocity, pressure, momentum, continuity, reaction, weight, mz_inverse):
    consts = [jnp.asarray(m) for m in operators()]
    any_spec = pl.BlockSpec(memory_space=pl.ANY)
    f32 = lambda *shape: pltpu.VMEM(shape, F32)
    b16 = lambda *shape: pltpu.VMEM(shape, BF16)
    flat = (ROWS, NY)
    scratch = [
        f32(3, *flat), f32(*flat), f32(3, *flat), f32(*flat), f32(*flat), f32(PX, NY), f32(40, 128),
        b16(2 * ROWS, DEPTH), b16(2 * ROWS, DEPTH), b16(NY, NY), b16(NY, NY), b16(NY, NY),
        f32(2, 3, HALO, NY), f32(2, 3, HALO, NY), f32(2, 3, EDGE, NY), f32(2, 3, EDGE, NY),
        f32(PX, 4 * PZ, NY), f32(PZ, NY), f32(8, NY), f32(8, NY),
        f32(*flat), f32(*flat), f32(*flat), f32(3, *flat), f32(3, *flat), f32(3, *flat),
        b16(DEPTH, NY), b16(DEPTH, NY), b16(16, NY), b16(16, NY), f32(8, NY),
        pltpu.SemaphoreType.DMA((16,)), pltpu.SemaphoreType.DMA((4,)),
        pltpu.SemaphoreType.DMA((64,)), pltpu.SemaphoreType.DMA((64,)),
    ]
    out, cor = pl.pallas_call(
        functools.partial(kernel, count_x),
        name="stokes",
        out_shape=[jax.ShapeDtypeStruct((3, *flat), F32), jax.ShapeDtypeStruct(flat, F32)],
        in_specs=[any_spec] * 12,
        out_specs=[any_spec] * 2,
        scratch_shapes=scratch,
        compiler_params=pltpu.CompilerParams(
            collective_id=0, has_side_effects=True, vmem_limit_bytes=48 << 20
        ),
    )(
        velocity.reshape(3, *flat), pressure.reshape(flat), momentum.reshape(3, *flat),
        continuity.reshape(flat), reaction.reshape(flat), weight, mz_inverse, *consts,
    )
    return out.reshape(3, PX, PZ, NY), cor.reshape(PX, PZ, NY)


def solution(mesh):
    return jax.shard_map(
        functools.partial(shards, mesh.shape["xy"]),
        mesh=mesh,
        in_specs=(
            P(None, "xy", "gz", None),
            P("xy", "gz", None),
            P(None, "xy", "gz", None),
            P("xy", "gz", None),
            P("xy", "gz", None),
            P("xy", None),
            P(),
        ),
        out_specs=(P(None, "xy", "gz", None), P("xy", "gz", None)),
        check_vma=False,
    )
```

time: 160 us -> 87.3 us (0.55)
  the two profiles are of different devices: /device:TPU:9 before, /device:TPU:1 now
where the time goes in v1:
time: 87.3 us; the launch traced here: 86.8 us
  Pallas kernels  72.9 us (84%)
  local copies, waits for them, and re-layouts  13.2 us (15%)
    pallas_call x1, Pallas kernels, shards(): pl.pallas_call(functools.partial(kernel, count_x), name='stokes', out_sha...  72.9 us
    unnamed x26, local copies, waits for them, and re-layouts  13.2 us

profile of v1, /device:TPU:1, one launch (start us, length us, event | category | flops | bytes accessed | tf_op | source)
XLA Modules:
  0.0 86.8 jit_solution(13441375060029827127)
XLA Ops:
  0.6 0.0 copy-start.11
  0.6 0.7 copy-done.11
  1.3 0.0 copy-start
  1.3 1.1 %copy-done = f32[3,4,32,512]{3,2,1,0:T(8,128)S(1)} copy-done((f32[3,4,32,512]{3,2,1,0:T(8,128)S(1)}, f32[3,4,32,512]{3,2,1,0:T(8,128)}, u32[]{:S(2)}) %copy-start) | copy-done | bytes 786456
  2.5 0.0 copy-start.1
  2.5 1.1 %copy-done.1 = f32[3,4,32,512]{3,2,1,0:T(8,128)S(1)} copy-done((f32[3,4,32,512]{3,2,1,0:T(8,128)S(1)}, f32[3,4,32,512]{3,2,1,0:T(8,128)}, u32[]{:S(2)}) %copy-start.1) | copy-done | bytes 786456
  3.6 0.0 copy-start.2
  3.6 1.0 %copy-done.2 = bf16[512,512]{1,0:T(8,128)(2,1)S(1)} copy-done((bf16[512,512]{1,0:T(8,128)(2,1)S(1)}, bf16[512,512]{1,0:T(8,128)(2,1)}, u32[]{:S(2)}) %copy-start.2) | copy-done | bytes 524312
  4.6 0.0 copy-start.3
  4.6 1.0 %copy-done.3 = bf16[512,512]{1,0:T(8,128)(2,1)S(1)} copy-done((bf16[512,512]{1,0:T(8,128)(2,1)S(1)}, bf16[512,512]{1,0:T(8,128)(2,1)}, u32[]{:S(2)}) %copy-start.3) | copy-done | bytes 524312
  5.7 0.0 copy-start.4
  5.7 1.0 %copy-done.4 = bf16[512,512]{1,0:T(8,128)(2,1)S(1)} copy-done((bf16[512,512]{1,0:T(8,128)(2,1)S(1)}, bf16[512,512]{1,0:T(8,128)(2,1)}, u32[]{:S(2)}) %copy-start.4) | copy-done | bytes 524312
  6.7 0.0 copy-start.5
  6.7 0.9 %copy-done.5 = f32[4,32,512]{2,1,0:T(8,128)S(1)} copy-done((f32[4,32,512]{2,1,0:T(8,128)S(1)}, f32[4,32,512]{2,1,0:T(8,128)}, u32[]{:S(2)}) %copy-start.5) | copy-done | bytes 262168
  7.7 0.0 copy-start.6
  7.7 0.9 %copy-done.6 = f32[4,32,512]{2,1,0:T(8,128)S(1)} copy-done((f32[4,32,512]{2,1,0:T(8,128)S(1)}, f32[4,32,512]{2,1,0:T(8,128)}, u32[]{:S(2)}) %copy-start.6) | copy-done | bytes 262168
  8.6 0.0 copy-start.7
  8.6 0.9 %copy-done.7 = f32[4,32,512]{2,1,0:T(8,128)S(1)} copy-done((f32[4,32,512]{2,1,0:T(8,128)S(1)}, f32[4,32,512]{2,1,0:T(8,128)}, u32[]{:S(2)}) %copy-start.7) | copy-done | bytes 262168
  9.6 0.0 copy-start.8
  9.6 0.9 %copy-done.8 = bf16[256,400]{1,0:T(8,128)(2,1)S(1)} copy-done((bf16[256,400]{1,0:T(8,128)(2,1)S(1)}, bf16[256,400]{1,0:T(8,128)(2,1)}, u32[]{:S(2)}) %copy-start.8) | copy-done | bytes 204824
  10.5 0.0 copy-start.9
  10.5 0.9 %copy-done.9 = bf16[256,400]{1,0:T(8,128)(2,1)S(1)} copy-done((bf16[256,400]{1,0:T(8,128)(2,1)S(1)}, bf16[256,400]{1,0:T(8,128)(2,1)}, u32[]{:S(2)}) %copy-start.9) | copy-done | bytes 204824
  11.5 0.0 copy-start.10
  11.5 0.8 copy-done.10
  12.3 72.9 %stokes.1 = (f32[3,128,512]{2,1,0:T(8,128)S(1)}, f32[128,512]{1,0:T(8,128)S(1)}) custom-call(f32[3,128,512]{2,1,0:T(8,128)S(1)} %bitcast.8, f32[128,512]{1,0:T(8,128)S(1)} %bitcast.10, f32[3,128,512]{2,1,0:T(8,128)S(1)} %bitcast.9, f32[128,512]{1,0:T(8,128)S(1)} %bitcast.11, f32[128,512]{1,0:T(8,128)S(1)} %bitcast.12, f32[4,512]{1,0:T(4,128)S(1)} %copy-done.11, ...), custom_call_target="tpu_custom_call" | custom-call | tf_op jit(solution)/shard_map/stokes/pallas_call | solution.py:400
  85.2 0.9 %copy.16 = f32[3,4,32,512]{3,2,1,0:T(8,128)} copy(f32[3,4,32,512]{3,2,1,0:T(8,128)S(1)} %bitcast.7) | data formatting | bytes 1572864
  86.1 0.7 copy.17
Async XLA Ops:
  0.6 0.7 copy-start.11
  1.3 1.1 %copy-start = (f32[3,4,32,512]{3,2,1,0:T(8,128)S(1)}, f32[3,4,32,512]{3,2,1,0:T(8,128)}, u32[]{:S(2)}) copy-start(f32[3,4,32,512]{3,2,1,0:T(8,128)} %param.12) | copy-start | bytes 2359300
  2.5 1.1 %copy-start.1 = (f32[3,4,32,512]{3,2,1,0:T(8,128)S(1)}, f32[3,4,32,512]{3,2,1,0:T(8,128)}, u32[]{:S(2)}) copy-start(f32[3,4,32,512]{3,2,1,0:T(8,128)} %param.14) | copy-start | bytes 2359300
  3.6 1.0 %copy-start.2 = (bf16[512,512]{1,0:T(8,128)(2,1)S(1)}, bf16[512,512]{1,0:T(8,128)(2,1)}, u32[]{:S(2)}) copy-start(bf16[512,512]{1,0:T(8,128)(2,1)} %constant.14.clone.ky_a) | copy-start | bytes 1572868
  4.6 1.0 %copy-start.3 = (bf16[512,512]{1,0:T(8,128)(2,1)S(1)}, bf16[512,512]{1,0:T(8,128)(2,1)}, u32[]{:S(2)}) copy-start(bf16[512,512]{1,0:T(8,128)(2,1)} %constant.13.clone.ml_a) | copy-start | bytes 1572868
  5.7 1.0 %copy-start.4 = (bf16[512,512]{1,0:T(8,128)(2,1)S(1)}, bf16[512,512]{1,0:T(8,128)(2,1)}, u32[]{:S(2)}) copy-start(bf16[512,512]{1,0:T(8,128)(2,1)} %constant.12.clone.mh_a) | copy-start | bytes 1572868
  6.7 0.9 %copy-start.5 = (f32[4,32,512]{2,1,0:T(8,128)S(1)}, f32[4,32,512]{2,1,0:T(8,128)}, u32[]{:S(2)}) copy-start(f32[4,32,512]{2,1,0:T(8,128)} %param.13) | copy-start | bytes 786436
  7.7 0.9 %copy-start.6 = (f32[4,32,512]{2,1,0:T(8,128)S(1)}, f32[4,32,512]{2,1,0:T(8,128)}, u32[]{:S(2)}) copy-start(f32[4,32,512]{2,1,0:T(8,128)} %param.15) | copy-start | bytes 786436
  8.6 0.9 %copy-start.7 = (f32[4,32,512]{2,1,0:T(8,128)S(1)}, f32[4,32,512]{2,1,0:T(8,128)}, u32[]{:S(2)}) copy-start(f32[4,32,512]{2,1,0:T(8,128)} %param.16) | copy-start | bytes 786436
  9.6 0.9 %copy-start.8 = (bf16[256,400]{1,0:T(8,128)(2,1)S(1)}, bf16[256,400]{1,0:T(8,128)(2,1)}, u32[]{:S(2)}) copy-start(bf16[256,400]{1,0:T(8,128)(2,1)} %constant.11.clone.sl_a) | copy-start | bytes 614404
  10.5 0.9 %copy-start.9 = (bf16[256,400]{1,0:T(8,128)(2,1)S(1)}, bf16[256,400]{1,0:T(8,128)(2,1)}, u32[]{:S(2)}) copy-start(bf16[256,400]{1,0:T(8,128)(2,1)} %constant.10.clone.sh_a) | copy-start | bytes 614404
  11.5 0.8 copy-start.10

commit v2 on v1

v2 whole, which is shorter than its diff:
```python
import functools

import jax
import jax.numpy as jnp
import ml_dtypes
import numpy as np
from jax import lax
from jax.experimental import pallas as pl
from jax.experimental.pallas import tpu as pltpu
from jax.sharding import PartitionSpec as P

MASS_INT = (1.0, 120.0, 1191.0, 2416.0, 1191.0, 120.0, 1.0)
STIFF_INT = (-1.0, -24.0, -15.0, 80.0, -15.0, -24.0, -1.0)
MASS_SCALE = 5040.0
STIFF_SCALE = 120.0
DAMPING = 0.5
CENTRE_DIAG = 3.0 * (2.0 / 3.0) * (151.0 / 315.0) ** 2

PX = 4
PZ = 32
ROWS = PX * PZ
NY = 512
HALO = 3 * PZ
EDGE = 80
DEPTH = ROWS + 2 * HALO + EDGE
MESH = pl.DeviceIdType.MESH
F32 = jnp.float32
BF16 = jnp.bfloat16


def split_np(matrix):
    high = matrix.astype(ml_dtypes.bfloat16)
    low = (matrix - high.astype(np.float64)).astype(ml_dtypes.bfloat16)
    return high, low


def source_points():
    points = [(p, z) for p in range(PX) for z in range(PZ)]
    points += [(p, z) for p in (-3, -2, -1) for z in range(PZ)]
    points += [(p, z) for p in (4, 5, 6) for z in range(PZ)]
    inner, outer = tuple(range(PX)), (-3, -2, -1, 4, 5, 6)
    for planes in (inner, outer):
        for first in (-4, PZ):
            points += [(p, first + j) for p in planes for j in range(4)]
    return points


def operators():
    mass = {o: w / MASS_SCALE for o, w in zip(range(-3, 4), MASS_INT)}
    stiff = {o: w / STIFF_SCALE for o, w in zip(range(-3, 4), STIFF_INT)}
    plane = np.zeros((2 * ROWS, DEPTH), np.float64)
    for column, (x_in, z_in) in enumerate(source_points()):
        for x_out in range(PX):
            for z_out in range(PZ):
                ox, oz = x_in - x_out, z_in - z_out
                if abs(ox) <= 3 and abs(oz) <= 3:
                    row = x_out * PZ + z_out
                    plane[row, column] = (mass[ox] * stiff[oz] + stiff[ox] * mass[oz]) / MASS_SCALE
                    plane[ROWS + row, column] = mass[ox] * mass[oz] / STIFF_SCALE
    mass_y = np.zeros((NY, NY), np.float64)
    stiff_y = np.zeros((NY, NY), np.float64)
    for offset in range(-3, 4):
        mass_y += np.diag(np.full(NY - abs(offset), MASS_INT[offset + 3]), -offset)
        stiff_y += np.diag(np.full(NY - abs(offset), STIFF_INT[offset + 3]), -offset)
    return split_np(plane) + split_np(mass_y) + split_np(stiff_y)[:1]


def split(values):
    high = values.astype(BF16)
    return high, (values - high.astype(F32)).astype(BF16)


def dot(left, right):
    return jnp.dot(left, right, preferred_element_type=F32)


def kernel(
    count_x,
    vel, prs, mom, con, rea, pwt, mzi, sh_a, sl_a, mh_a, ml_a, ky_a,
    out, cor,
    V, PR, MS, CS, RE, PW, MZ, SH, SL, MH, ML, KY,
    XL, XR, ZB, PK, SG, QH, PD, PP, Q, CO, H, BASE, FS, OB, BH, BL, FW, QL,
    local_sem, out_sem, send_sem, recv_sem,
):
    i = lax.axis_index("xy")
    g = lax.axis_index("gz")
    half = count_x // 2
    left = (lax.rem(i + count_x - 1, count_x), g)
    right = (lax.rem(i + 1, count_x), g)
    upper = (i, lax.rem(g + 1, 4))
    lower = (i, lax.rem(g + 3, 4))
    across = (i, lax.rem(g + 2, 4))
    core = (i, g + 1 - 2 * lax.rem(g, 2))
    has_left, has_right = i > 0, i < count_x - 1
    has_lower, has_upper = g > 0, g < 3
    at_low, at_high = i == half - 1, i == half
    at_middle = jnp.logical_or(at_low, at_high)
    elsewhere = jnp.logical_not(at_middle)
    left_direct = jnp.logical_and(has_left, i != half)
    right_direct = jnp.logical_and(has_right, i != half - 1)

    loads = []

    def load(src, dst):
        copy = pltpu.make_async_copy(src, dst, local_sem.at[len(loads)])
        copy.start()
        loads.append(copy)
        return copy

    load_v = {c: load(vel.at[c], V.at[c]) for c in (2, 0, 1)}
    load_p = load(prs, PR)
    load_c = load(con, CS)
    load_w = load(pwt, PW)
    load_z = load(mzi.at[pl.ds(pl.multiple_of(g * PZ, PZ), PZ)], MZ.at[pl.ds(8, PZ)])
    load_r = load(rea, RE)
    load_ops = [load(a, b) for a, b in ((sh_a, SH), (sl_a, SL), (mh_a, MH), (ml_a, ML), (ky_a, KY))]
    load_m = load(mom, MS)
    above = pl.multiple_of(jnp.maximum(g * PZ - 8, 0), 8)
    load_z2 = pltpu.make_async_copy(mzi.at[pl.ds(above, 8)], MZ.at[pl.ds(0, 8)], local_sem.at[len(loads)])

    barrier = pltpu.get_barrier_semaphore()
    for device in (upper, lower, across):
        pl.semaphore_signal(barrier, inc=1, device_id=device, device_id_type=MESH)

    def greet(condition, *devices):
        @pl.when(condition)
        def _():
            for device in devices:
                pl.semaphore_signal(barrier, inc=1, device_id=device, device_id_type=MESH)

        return len(devices) * condition.astype(jnp.int32)

    greeted = greet(has_left, left) + greet(has_right, right)
    greeted += greet(at_middle, (0, g), (count_x - 1, g))
    greeted += greet(i == 0, (half - 1, g), (half, g))
    greeted += greet(i == count_x - 1, (half - 1, g), (half, g))

    @pl.when(has_lower)
    def _():
        load_z2.start()

    @pl.when(jnp.logical_not(has_left))
    def _():
        XL[...] = jnp.zeros_like(XL)
        QH[...] = jnp.zeros_like(QH)

    @pl.when(jnp.logical_not(has_right))
    def _():
        XR[...] = jnp.zeros_like(XR)

    @pl.when(jnp.logical_not(has_lower))
    def _():
        MZ[0:8, :] = jnp.zeros((8, 128), F32)
        PD[...] = jnp.zeros_like(PD)
        for s in range(2):
            for c in range(3):
                ZB[s, c, 0:16, :] = jnp.zeros((16, NY), F32)
                ZB[s, c, 32:56, :] = jnp.zeros((24, NY), F32)

    @pl.when(jnp.logical_not(has_upper))
    def _():
        for s in range(2):
            for c in range(3):
                ZB[s, c, 16:32, :] = jnp.zeros((16, NY), F32)
                ZB[s, c, 56:80, :] = jnp.zeros((24, NY), F32)

    used = [0]
    started = []

    def remote(src, dst, device, sends, receives, counts=None):
        at = used[0]
        used[0] += 1
        copy = pltpu.make_async_remote_copy(
            src_ref=src, dst_ref=dst, send_sem=send_sem.at[at],
            recv_sem=recv_sem.at[at if counts is None else counts[3]],
            device_id=device, device_id_type=MESH,
        )
        started.append((copy, sends))
        return copy, sends, receives, at

    def guarded(condition, actions):
        if condition is None:
            for action in actions:
                action()
        else:

            @pl.when(condition)
            def _():
                for action in actions:
                    action()

    def start(*copies):
        guarded(copies[0][1], [copy[0].start for copy in copies])

    def arrive(*copies):
        guarded(copies[0][2], [copy[0].wait_recv for copy in copies])

    def to_left(src, dst, direct=True):
        return remote(src, dst, left, has_left if direct else left_direct, has_right)

    def to_right(src, dst, direct=True):
        return remote(src, dst, right, has_right if direct else right_direct, has_left)

    def to_upper(src, dst):
        return remote(src, dst, upper, has_upper, has_lower)

    def to_lower(src, dst):
        return remote(src, dst, lower, has_lower, has_upper)

    def both_ways(s, c, ref, first=0, rows=pl.ds(0, PZ)):
        lefts = (ref.at[c, pl.ds(first, 3 - first), rows], XR.at[s, c, pl.ds(first, 3 - first), rows])
        rights = (ref.at[c, pl.ds(1, 3), rows], XL.at[s, c, :, rows])
        return to_left(*lefts), to_right(*rights)

    def start_late(pair):
        pl.when(left_direct)(pair[0][0].start)
        pl.when(right_direct)(pair[1][0].start)

        def later():
            pl.when(at_high)(pair[0][0].start)
            pl.when(at_low)(pair[1][0].start)

        return later

    def by_planes(s, c, ref):
        pairs, hand_on = [], []
        for p in range(3):
            slot = FW.at[s, p]
            source_l, target_l = ref.at[c, p], XR.at[s, c, p]
            source_r, target_r = ref.at[c, p + 1], XL.at[s, c, p]
            go_l, go_r = to_left(source_l, target_l, False), to_right(source_r, target_r, False)
            out_l = remote(source_l, slot, (0, g), at_high, i == 0)
            out_r = remote(source_r, slot, (count_x - 1, g), at_low, i == count_x - 1)
            on_l = remote(slot, target_l, (half - 1, g), i == 0, None, go_l)
            on_r = remote(slot, target_r, (half, g), i == count_x - 1, None, go_r)
            pairs += [go_l, go_r]
            for copy in (go_l, go_r, out_l, out_r):
                start(copy)
            hand_on.append(((out_l, on_l), (out_r, on_r)))

        def pass_on(p):
            for arriving, leaving in hand_on[p]:
                guarded(leaving[1], [arriving[0].wait_recv, leaving[0].start])

        return pairs, pass_on

    pl.semaphore_wait(barrier, 3 + greeted)

    v_first = to_left(vel.at[0, 0], XR.at[0, 0, 0])
    start(v_first)
    v_halo = {}
    v_halo[1], v_pass = by_planes(0, 1, vel)
    v_halo[2] = both_ways(0, 2, vel)
    v2_later = start_late(v_halo[2])
    v_halo[0] = both_ways(0, 0, vel, 1)
    v0_later = start_late(v_halo[0])

    def edges(s, c, ref):
        for p in range(PX):
            PK[s, c, pl.ds(4 * p, 4), :] = ref[c, p, pl.ds(PZ - 4, 4), :]
            PK[s, c, pl.ds(16 + 4 * p, 4), :] = ref[c, p, pl.ds(0, 4), :]
        down = to_lower(PK.at[s, c, pl.ds(16, 16)], ZB.at[s, c, pl.ds(16, 16)])
        up = to_upper(PK.at[s, c, pl.ds(0, 16)], ZB.at[s, c, pl.ds(0, 16)])
        start(down)
        start(up)
        return down, up

    def corners(s, c):
        down = to_lower(PK.at[s, c, pl.ds(56, 24)], ZB.at[s, c, pl.ds(56, 24)])
        up = to_upper(PK.at[s, c, pl.ds(32, 24)], ZB.at[s, c, pl.ds(32, 24)])

        def send(halo):
            for copy in halo:
                arrive(copy)
            for side, ref in enumerate((XL, XR)):
                for p in range(3):
                    at = 12 * side + 4 * p
                    PK[s, c, pl.ds(32 + at, 4), :] = ref[s, c, p, pl.ds(PZ - 4, 4), :]
                    PK[s, c, pl.ds(56 + at, 4), :] = ref[s, c, p, pl.ds(0, 4), :]
            start(down)
            start(up)

        return (down, up), send

    edge, corner, send_corner = {}, {}, {}
    for s in range(2):
        for c in range(3):
            corner[s, c], send_corner[s, c] = corners(s, c)

    def arrive_z(s, c):
        for j in range(2):
            if (s, c, j) != (0, 2, 0):
                arrive(edge[s, c][j])
            arrive(corner[s, c][j])

    load_v[2].wait()
    edge[0, 2] = edges(0, 2, V)
    load_p.wait()
    for p in range(PX):
        PP[pl.ds(p, 1), :] = PR[p, pl.ds(PZ - 1, 1), :]
    PP[pl.ds(4, 4), :] = jnp.zeros((4, NY), F32)
    p_rows = to_upper(PP, PD)
    start(p_rows)
    load_v[0].wait()
    load_v[1].wait()
    edge[0, 1] = edges(0, 1, V)
    edge[0, 0] = edges(0, 0, V)

    row_at = lax.broadcasted_iota(jnp.int32, (PZ, NY), 0)
    lane_at = lax.broadcasted_iota(jnp.int32, (PZ, NY), 1)

    mine = pl.ds(pl.multiple_of(g * PZ, PZ), PZ)
    theirs = pl.ds(pl.multiple_of(lax.rem(g + 2, 4) * PZ, PZ), PZ)
    s_across = [remote(SG.at[p, mine], SG.at[p, mine], across, None, None) for p in range(PX)]
    s_core = [remote(SG.at[p, mine], SG.at[p, mine], core, None, None) for p in range(PX)]
    s_next = [remote(SG.at[p, theirs], SG.at[p, theirs], core, None, None) for p in range(PX)]

    def residual(p):
        vx, vy, vz = (V[c, p] for c in range(3))
        next_x = XR[0, 0, 0] if p == PX - 1 else V[0, p + 1]
        next_y = jnp.where(lane_at == NY - 1, 0.0, pltpu.roll(vy, NY - 1, 1))
        beyond = ZB[0, 2, pl.ds(16 + 4 * p, 1), :]
        next_z = jnp.where(row_at == PZ - 1, beyond, pltpu.roll(vz, PZ - 1, 0))
        diverged = (next_x - vx) + (next_y - vy) + (next_z - vz)
        SG[p, mine, :] = -PW[pl.ds(p, 1), :] * (CS[p] - diverged)
        start(s_across[p], s_core[p])

    load_c.wait()
    load_w.wait()
    arrive(edge[0, 2][0])
    for p in range(PX - 1):
        residual(p)
    arrive(v_first)
    residual(PX - 1)
    v_pass(0)

    load_r.wait()
    H[...] = DAMPING / (CENTRE_DIAG + RE[...])
    for copy in load_ops:
        copy.wait()
    load_m.wait()
    load_z.wait()

    @pl.when(has_lower)
    def _():
        load_z2.wait()

    def flat(values):
        return values.reshape(-1, NY)

    def operate(s, c, ref):
        BH[0:ROWS, :], BL[0:ROWS, :] = split(flat(ref[c]))
        BH[ROWS:ROWS + HALO, :], BL[ROWS:ROWS + HALO, :] = split(flat(XL[s, c]))
        BH[ROWS + HALO:ROWS + 2 * HALO, :], BL[ROWS + HALO:ROWS + 2 * HALO, :] = split(flat(XR[s, c]))
        BH[ROWS + 2 * HALO:, :], BL[ROWS + 2 * HALO:, :] = split(ZB[s, c])
        both = dot(SH[...], BH[...]) + (dot(SL[...], BH[...]) + dot(SH[...], BL[...]))
        first_h, first_l = split(both[:ROWS])
        second_h, second_l = split(both[ROWS:])
        mass, stiff = MH[...], KY[...]
        return ((dot(first_h, mass) + dot(second_h, stiff)) + (
            dot(first_l, mass) + dot(second_l, stiff) + dot(first_h, ML[...])
        )).reshape(PX, PZ, NY)

    def base(c):
        BASE[c] = MS[c] - operate(0, c, V) - RE[...] * V[c]

    mz_h, mz_l = split(MZ[...])

    def solve(p):
        s_h, s_l = split(SG[p])
        solved = dot(mz_h, s_h) + (dot(mz_l, s_h) + dot(mz_h, s_l))
        CO[p] = solved[8:]
        Q[p] = solved[8:] + PR[p]
        QL[pl.ds(p, 1), :] = solved[7:8] + PD[pl.ds(p, 1), :]

    def sweep(c):
        for p in range(PX):
            q = Q[p]
            if c == 0:
                before = QH[...] if p == 0 else Q[p - 1]
            elif c == 1:
                before = jnp.where(lane_at == 0, 0.0, pltpu.roll(q, 1, 1))
            else:
                before = jnp.where(row_at == 0, QL[pl.ds(p, 1), :], pltpu.roll(q, 1, 0))
            FS[c, p] = H[p] * (BASE[c, p] - (before - q))

    v_pass(1)
    v_pass(2)
    for p in range(2):
        arrive(s_across[p])
        start(s_next[p])
    send_corner[0, 1](v_halo[1])
    for p in range(2, PX):
        arrive(s_across[p])
        start(s_next[p])
    v2_later()
    pl.when(elsewhere)(lambda: send_corner[0, 2](v_halo[2]))
    arrive_z(0, 1)
    base(1)
    arrive(p_rows)
    for p in reversed(range(PX)):
        arrive(s_core[p], s_next[p])
        solve(p)
    q_plane = to_right(Q.at[PX - 1], QH)
    start(q_plane)
    c_out = pltpu.make_async_copy(CO, cor, out_sem.at[3])
    c_out.start()
    f_halo = {}
    sweep(1)
    f_halo[1], f_pass = by_planes(1, 1, FS)
    edge[1, 1] = edges(1, 1, FS)
    pl.when(at_middle)(lambda: send_corner[0, 2](v_halo[2]))
    v0_later()
    arrive_z(0, 2)
    base(2)
    sweep(2)
    f_halo[2] = both_ways(1, 2, FS)
    start(f_halo[2][0])
    start(f_halo[2][1])
    edge[1, 2] = edges(1, 2, FS)
    send_corner[0, 0](v_halo[0])
    f_pass(0)
    arrive_z(0, 0)
    base(0)
    arrive(q_plane)
    sweep(0)
    f_ends = both_ways(1, 0, FS, rows=pl.ds(0, 8)) + both_ways(1, 0, FS, rows=pl.ds(24, 8))
    f_rest = both_ways(1, 0, FS, rows=pl.ds(8, 16))
    for copy in f_ends + f_rest:
        start(copy)
    edge[1, 0] = edges(1, 0, FS)
    f_pass(1)
    f_pass(2)

    outs = []

    def finish(c):
        OB[c] = FS[c] * (2.0 - RE[...] * H[...]) - H[...] * operate(1, c, FS)
        copy = pltpu.make_async_copy(OB.at[c], out.at[c], out_sem.at[c])
        copy.start()
        outs.append(copy)

    send_corner[1, 1](f_halo[1])
    arrive_z(1, 1)
    finish(1)
    send_corner[1, 2](f_halo[2])
    send_corner[1, 0](f_ends)
    arrive_z(1, 2)
    finish(2)
    for copy in f_rest:
        arrive(copy)
    arrive_z(1, 0)
    finish(0)

    for copy, sends in started:
        guarded(sends, [copy.wait_send])
    c_out.wait()
    for copy in outs:
        copy.wait()


def shards(count_x, velocity, pressure, momentum, continuity, reaction, weight, mz_inverse):
    consts = [jnp.asarray(m) for m in operators()]
    any_spec = pl.BlockSpec(memory_space=pl.ANY)
    f32 = lambda *shape: pltpu.VMEM(shape, F32)
    b16 = lambda *shape: pltpu.VMEM(shape, BF16)
    grid = (PX, PZ, NY)
    halo = (2, 3, 3, PZ, NY)
    scratch = [
        f32(3, *grid), f32(*grid), f32(3, *grid), f32(*grid), f32(*grid), f32(PX, NY), f32(40, 128),
        b16(2 * ROWS, DEPTH), b16(2 * ROWS, DEPTH), b16(NY, NY), b16(NY, NY), b16(NY, NY),
        f32(*halo), f32(*halo), f32(2, 3, EDGE, NY), f32(2, 3, EDGE, NY),
        f32(PX, 4 * PZ, NY), f32(PZ, NY), f32(8, NY), f32(8, NY),
        f32(*grid), f32(*grid), f32(*grid), f32(3, *grid), f32(3, *grid), f32(3, *grid),
        b16(DEPTH, NY), b16(DEPTH, NY), f32(2, 3, PZ, NY), f32(8, NY),
        pltpu.SemaphoreType.DMA((16,)), pltpu.SemaphoreType.DMA((4,)),
        pltpu.SemaphoreType.DMA((128,)), pltpu.SemaphoreType.DMA((128,)),
    ]
    return pl.pallas_call(
        functools.partial(kernel, count_x),
        name="stokes",
        out_shape=[jax.ShapeDtypeStruct((3, *grid), F32), jax.ShapeDtypeStruct(grid, F32)],
        in_specs=[pl.BlockSpec(memory_space=pltpu.HBM)] * 12,
        out_specs=[any_spec] * 2,
        scratch_shapes=scratch,
        compiler_params=pltpu.CompilerParams(
            collective_id=0, has_side_effects=True, vmem_limit_bytes=62 << 20
        ),
    )(velocity, pressure, momentum, continuity, reaction, weight, mz_inverse, *consts)


def solution(mesh):
    return jax.shard_map(
        functools.partial(shards, mesh.shape["xy"]),
        mesh=mesh,
        in_specs=(
            P(None, "xy", "gz", None),
            P("xy", "gz", None),
            P(None, "xy", "gz", None),
            P("xy", "gz", None),
            P("xy", "gz", None),
            P("xy", None),
            P(),
        ),
        out_specs=(P(None, "xy", "gz", None), P("xy", "gz", None)),
        check_vma=False,
    )
```

time: 87.3 us -> 59.4 us (0.68)
  Pallas kernels: 72.9 us -> 55.8 us
  local copies, waits for them, and re-layouts: 13.2 us -> 2.81 us
    pallas_call x1, Pallas kernels: 72.9 us -> 55.8 us  [shards(): pl.pallas_call(functools.partial(kernel, count_x), name='stokes', out_sha...]
    unnamed x26 -> x4, local copies, waits for them, and re-layouts: 13.2 us -> 2.81 us
where the time goes in v2:
time: 59.4 us; the launch traced here: 59.2 us
  Pallas kernels  55.8 us (94%)
  local copies, waits for them, and re-layouts  2.81 us (5%)
  between operations  0.65 us (1%)
    pallas_call x1, Pallas kernels, shards(): pl.pallas_call(functools.partial(kernel, count_x), name='stokes', out_sha...  55.8 us
    unnamed x4, local copies, waits for them, and re-layouts  2.81 us

profile of v2, /device:TPU:1, one launch (start us, length us, event | category | flops | bytes accessed | tf_op | source)
XLA Modules:
  0.0 59.2 jit_solution(17828618641631600963)
XLA Ops:
  0.6 55.8 %stokes.1 = (f32[3,4,32,512]{3,2,1,0:T(8,128)}, f32[4,32,512]{2,1,0:T(8,128)}) custom-call(f32[3,4,32,512]{3,2,1,0:T(8,128)} %vel.1, f32[4,32,512]{2,1,0:T(8,128)} %prs.1, f32[3,4,32,512]{3,2,1,0:T(8,128)} %mom.1, f32[4,32,512]{2,1,0:T(8,128)} %con.1, f32[4,32,512]{2,1,0:T(8,128)} %rea.1, f32[4,512]{1,0:T(4,128)} %pwt.1, f32[128,128]{1,0:T(8,128)} %mzi.1, ...), custom_call_target="tpu_custom_call" | custom-call | tf_op jit(solution)/shard_map/stokes/pallas_call | solution.py:479
  56.4 0.0 copy-start
  56.4 2.1 %copy.16 = f32[3,4,32,512]{3,2,1,0:T(8,128)} copy(f32[3,4,32,512]{3,2,1,0:T(8,128)} %get-tuple-element.4) | data formatting | bytes 1572864
  58.5 0.0 copy-done
  58.5 0.7 %copy.17 = f32[4,32,512]{2,1,0:T(8,128)} copy(f32[4,32,512]{2,1,0:T(8,128)S(1)} %copy-done) | data formatting | bytes 524288
Async XLA Ops:
  56.4 2.1 %copy-start = (f32[4,32,512]{2,1,0:T(8,128)S(1)}, f32[4,32,512]{2,1,0:T(8,128)}, u32[]{:S(2)}) copy-start(f32[4,32,512]{2,1,0:T(8,128)} %get-tuple-element.5) | copy-start | bytes 786436

commit v3 on v2

--- a/solution.py
+++ b/solution.py
@@ -22,7 +22,8 @@
 NY = 512
 HALO = 3 * PZ
 EDGE = 80
-DEPTH = ROWS + 2 * HALO + EDGE
+NEAR = ROWS + 32
+FAR = 2 * HALO + 48
 MESH = pl.DeviceIdType.MESH
 F32 = jnp.float32
 BF16 = jnp.bfloat16
@@ -35,21 +36,25 @@
 
 
 def source_points():
-    points = [(p, z) for p in range(PX) for z in range(PZ)]
-    points += [(p, z) for p in (-3, -2, -1) for z in range(PZ)]
-    points += [(p, z) for p in (4, 5, 6) for z in range(PZ)]
-    inner, outer = tuple(range(PX)), (-3, -2, -1, 4, 5, 6)
-    for planes in (inner, outer):
-        for first in (-4, PZ):
-            points += [(p, first + j) for p in planes for j in range(4)]
-    return points
+    inner, left, right = tuple(range(PX)), (-3, -2, -1), (4, 5, 6)
+
+    def ends(planes):
+        return [(p, first + j) for first in (-4, PZ) for p in planes for j in range(4)]
+
+    near = [(p, z) for p in inner for z in range(PZ)] + ends(inner)
+    far = [(p, z) for p in left + right for z in range(PZ)] + ends(left + right)
+    return near + [None] * (256 - len(near)) + far
 
 
 def operators():
     mass = {o: w / MASS_SCALE for o, w in zip(range(-3, 4), MASS_INT)}
     stiff = {o: w / STIFF_SCALE for o, w in zip(range(-3, 4), STIFF_INT)}
-    plane = np.zeros((2 * ROWS, DEPTH), np.float64)
-    for column, (x_in, z_in) in enumerate(source_points()):
+    points = source_points()
+    plane = np.zeros((2 * ROWS, len(points)), np.float64)
+    for column, point in enumerate(points):
+        if point is None:
+            continue
+        x_in, z_in = point
         for x_out in range(PX):
             for z_out in range(PZ):
                 ox, oz = x_in - x_out, z_in - z_out
@@ -62,7 +67,17 @@
     for offset in range(-3, 4):
         mass_y += np.diag(np.full(NY - abs(offset), MASS_INT[offset + 3]), -offset)
         stiff_y += np.diag(np.full(NY - abs(offset), STIFF_INT[offset + 3]), -offset)
-    return split_np(plane) + split_np(mass_y) + split_np(stiff_y)[:1]
+    half = NY // 2
+
+    def halves(matrix):
+        low = slice(half // 2, half + half // 2)
+        across = matrix[low, low].copy()
+        across[:half // 2, :half // 2] = 0
+        across[half // 2:, half // 2:] = 0
+        return np.stack([matrix[:half, :half], across])
+
+    mass_h, mass_l = split_np(halves(mass_y))
+    return split_np(plane) + (mass_h, mass_l, split_np(halves(stiff_y))[0])
 
 
 def split(values):
@@ -79,7 +94,7 @@
     vel, prs, mom, con, rea, pwt, mzi, sh_a, sl_a, mh_a, ml_a, ky_a,
     out, cor,
     V, PR, MS, CS, RE, PW, MZ, SH, SL, MH, ML, KY,
-    XL, XR, ZB, PK, SG, QH, PD, PP, Q, CO, H, BASE, FS, OB, BH, BL, FW, QL,
+    XL, XR, ZB, PK, SG, QH, PD, PP, Q, CO, H, BASE, FS, OB, NH, NL, BH, BL, TE, FW, QL,
     local_sem, out_sem, send_sem, recv_sem,
 ):
     i = lax.axis_index("xy")
@@ -98,6 +113,9 @@
     elsewhere = jnp.logical_not(at_middle)
     left_direct = jnp.logical_and(has_left, i != half)
     right_direct = jnp.logical_and(has_right, i != half - 1)
+    at_first, at_last = i == 0, i == count_x - 1
+    step = 8 if count_x > 16 else 1
+    at_low_side, at_high_side = i == step - 1, i == count_x - step
 
     loads = []
 
@@ -131,7 +149,9 @@
         return len(devices) * condition.astype(jnp.int32)
 
     greeted = greet(has_left, left) + greet(has_right, right)
-    greeted += greet(at_middle, (0, g), (count_x - 1, g))
+    greeted += greet(at_middle, (0, g), (count_x - 1, g), (step - 1, g), (count_x - step, g))
+    greeted += greet(at_low_side, (half - 1, g), (half, g))
+    greeted += greet(at_high_side, (half - 1, g), (half, g))
     greeted += greet(i == 0, (half - 1, g), (half, g))
     greeted += greet(i == count_x - 1, (half - 1, g), (half, g))
 
@@ -195,11 +215,15 @@
     def arrive(*copies):
         guarded(copies[0][2], [copy[0].wait_recv for copy in copies])
 
-    def to_left(src, dst, direct=True):
-        return remote(src, dst, left, has_left if direct else left_direct, has_right)
-
-    def to_right(src, dst, direct=True):
-        return remote(src, dst, right, has_right if direct else right_direct, has_left)
+    def to_left(src, dst, direct=False):
+        if direct:
+            return remote(src, dst, left, has_left, has_right)
+        return remote(src, dst, left, left_direct, right_direct)
+
+    def to_right(src, dst, direct=False):
+        if direct:
+            return remote(src, dst, right, has_right, has_left)
+        return remote(src, dst, right, right_direct, left_direct)
 
     def to_upper(src, dst):
         return remote(src, dst, upper, has_upper, has_lower)
@@ -207,53 +231,51 @@
     def to_lower(src, dst):
         return remote(src, dst, lower, has_lower, has_upper)
 
-    def both_ways(s, c, ref, first=0, rows=pl.ds(0, PZ)):
+    def both_ways(s, c, ref, first=0, rows=pl.ds(0, PZ), direct=False):
         lefts = (ref.at[c, pl.ds(first, 3 - first), rows], XR.at[s, c, pl.ds(first, 3 - first), rows])
         rights = (ref.at[c, pl.ds(1, 3), rows], XL.at[s, c, :, rows])
-        return to_left(*lefts), to_right(*rights)
-
-    def start_late(pair):
-        pl.when(left_direct)(pair[0][0].start)
-        pl.when(right_direct)(pair[1][0].start)
-
-        def later():
-            pl.when(at_high)(pair[0][0].start)
-            pl.when(at_low)(pair[1][0].start)
-
-        return later
-
-    def by_planes(s, c, ref):
-        pairs, hand_on = [], []
+        pair = to_left(*lefts, direct), to_right(*rights, direct)
+        for copy in pair:
+            start(copy)
+        return pair
+
+    def middle(s, c, ref, turns, first=0, now=True):
+        ends = ((0, at_first), (count_x - 1, at_last))
+        sides = ((step - 1, at_low_side), (count_x - step, at_high_side))
+        hops = []
         for p in range(3):
-            slot = FW.at[s, p]
-            source_l, target_l = ref.at[c, p], XR.at[s, c, p]
-            source_r, target_r = ref.at[c, p + 1], XL.at[s, c, p]
-            go_l, go_r = to_left(source_l, target_l, False), to_right(source_r, target_r, False)
-            out_l = remote(source_l, slot, (0, g), at_high, i == 0)
-            out_r = remote(source_r, slot, (count_x - 1, g), at_low, i == count_x - 1)
-            on_l = remote(slot, target_l, (half - 1, g), i == 0, None, go_l)
-            on_r = remote(slot, target_r, (half, g), i == count_x - 1, None, go_r)
-            pairs += [go_l, go_r]
-            for copy in (go_l, go_r, out_l, out_r):
-                start(copy)
-            hand_on.append(((out_l, on_l), (out_r, on_r)))
-
-        def pass_on(p):
-            for arriving, leaving in hand_on[p]:
-                guarded(leaving[1], [arriving[0].wait_recv, leaving[0].start])
-
-        return pairs, pass_on
+            by_left, by_right = sides if turns[p] == 2 else (ends[turns[p]], ends[1 - turns[p]])
+            slot = FW.at[s, c, p]
+            hop = []
+            if p >= first:
+                out = remote(ref.at[c, p], slot, (by_left[0], g), at_high, by_left[1])
+                hop.append((out, remote(slot, XR.at[s, c, p], (half - 1, g), by_left[1], at_low)))
+            out = remote(ref.at[c, p + 1], slot, (by_right[0], g), at_low, by_right[1])
+            hop.append((out, remote(slot, XL.at[s, c, p], (half, g), by_right[1], at_high)))
+            hops.append(hop)
+
+        def pass_on(*planes):
+            for p in planes:
+                for out, on in hops[p]:
+                    guarded(on[1], [out[0].wait_recv, on[0].start])
+
+        def send():
+            for hop in hops:
+                for out, _ in hop:
+                    start(out)
+
+        if now:
+            send()
+        return tuple(on for hop in hops for _, on in hop), pass_on, send
 
     pl.semaphore_wait(barrier, 3 + greeted)
 
-    v_first = to_left(vel.at[0, 0], XR.at[0, 0, 0])
+    v_first = to_left(vel.at[0, 0], XR.at[0, 0, 0], True)
     start(v_first)
-    v_halo = {}
-    v_halo[1], v_pass = by_planes(0, 1, vel)
-    v_halo[2] = both_ways(0, 2, vel)
-    v2_later = start_late(v_halo[2])
-    v_halo[0] = both_ways(0, 0, vel, 1)
-    v0_later = start_late(v_halo[0])
+    v_halo, v_pass, f_halo, f_pass = {}, {}, {}, {}
+    for c, turns, first in ((1, (2, 2, 2), 0), (2, (1, 1, 1), 0), (0, (0, 0, 0), 1)):
+        across_middle, v_pass[c], v_send = middle(0, c, vel, turns, first, c > 0)
+        v_halo[c] = both_ways(0, c, vel, first) + across_middle
 
     def edges(s, c, ref):
         for p in range(PX):
@@ -286,12 +308,6 @@
     for s in range(2):
         for c in range(3):
             corner[s, c], send_corner[s, c] = corners(s, c)
-
-    def arrive_z(s, c):
-        for j in range(2):
-            if (s, c, j) != (0, 2, 0):
-                arrive(edge[s, c][j])
-            arrive(corner[s, c][j])
 
     load_v[2].wait()
     edge[0, 2] = edges(0, 2, V)
@@ -332,7 +348,7 @@
         residual(p)
     arrive(v_first)
     residual(PX - 1)
-    v_pass(0)
+    v_pass[1](0)
 
     load_r.wait()
     H[...] = DAMPING / (CENTRE_DIAG + RE[...])
@@ -348,23 +364,48 @@
     def flat(values):
         return values.reshape(-1, NY)
 
-    def operate(s, c, ref):
-        BH[0:ROWS, :], BL[0:ROWS, :] = split(flat(ref[c]))
-        BH[ROWS:ROWS + HALO, :], BL[ROWS:ROWS + HALO, :] = split(flat(XL[s, c]))
-        BH[ROWS + HALO:ROWS + 2 * HALO, :], BL[ROWS + HALO:ROWS + 2 * HALO, :] = split(flat(XR[s, c]))
-        BH[ROWS + 2 * HALO:, :], BL[ROWS + 2 * HALO:, :] = split(ZB[s, c])
-        both = dot(SH[...], BH[...]) + (dot(SL[...], BH[...]) + dot(SH[...], BL[...]))
-        first_h, first_l = split(both[:ROWS])
-        second_h, second_l = split(both[ROWS:])
-        mass, stiff = MH[...], KY[...]
-        return ((dot(first_h, mass) + dot(second_h, stiff)) + (
-            dot(first_l, mass) + dot(second_l, stiff) + dot(first_h, ML[...])
-        )).reshape(PX, PZ, NY)
+    def plane_part(columns, high, low):
+        return dot(SH[:, columns], high) + (dot(SL[:, columns], high) + dot(SH[:, columns], low))
+
+    def near_part(s, c, ref):
+        for j in range(2):
+            if (s, c, j) != (0, 2, 0):
+                arrive(edge[s, c][j])
+        NH[0:ROWS, :], NL[0:ROWS, :] = split(flat(ref[c]))
+        NH[ROWS:, :], NL[ROWS:, :] = split(ZB[s, c, 0:32])
+        TE[c] = plane_part(slice(0, NEAR), NH[...], NL[...])
+
+    def along_y(first, second):
+        parts = split(first) + split(second)
+
+        def product(at, cut):
+            first_h, first_l, second_h, second_l = (cut(part) for part in parts)
+            mass, stiff = MH[at], KY[at]
+            return (dot(first_h, mass) + dot(second_h, stiff)) + (
+                dot(first_l, mass) + dot(second_l, stiff) + dot(first_h, ML[at])
+            )
+
+        main = product(0, lambda a: jnp.concatenate([a[:, :256], a[:, 256:]], axis=0))
+        cross = product(1, lambda a: a[:, 128:384])
+        return jnp.concatenate(
+            [main[:ROWS, :128], main[:ROWS, 128:] + cross[:, :128],
+             main[ROWS:, :128] + cross[:, 128:], main[ROWS:, 128:]], axis=1
+        )
+
+    def operate(s, c):
+        for j in range(2):
+            arrive(corner[s, c][j])
+        BH[0:HALO, :], BL[0:HALO, :] = split(flat(XL[s, c]))
+        BH[HALO:2 * HALO, :], BL[HALO:2 * HALO, :] = split(flat(XR[s, c]))
+        BH[2 * HALO:, :], BL[2 * HALO:, :] = split(ZB[s, c, 32:80])
+        both = TE[c] + plane_part(slice(256, 256 + FAR), BH[...], BL[...])
+        return along_y(both[:ROWS], both[ROWS:]).reshape(PX, PZ, NY)
 
     def base(c):
-        BASE[c] = MS[c] - operate(0, c, V) - RE[...] * V[c]
+        BASE[c] = MS[c] - operate(0, c) - RE[...] * V[c]
 
     mz_h, mz_l = split(MZ[...])
+    near_part(0, 1, V)
 
     def solve(p):
         s_h, s_l = split(SG[p])
@@ -384,72 +425,67 @@
                 before = jnp.where(row_at == 0, QL[pl.ds(p, 1), :], pltpu.roll(q, 1, 0))
             FS[c, p] = H[p] * (BASE[c, p] - (before - q))
 
-    v_pass(1)
-    v_pass(2)
+    v_pass[1](1, 2)
     for p in range(2):
         arrive(s_across[p])
         start(s_next[p])
     send_corner[0, 1](v_halo[1])
+    near_part(0, 2, V)
     for p in range(2, PX):
         arrive(s_across[p])
         start(s_next[p])
-    v2_later()
+    v_send()
+    v_pass[2](0, 1, 2)
     pl.when(elsewhere)(lambda: send_corner[0, 2](v_halo[2]))
-    arrive_z(0, 1)
+    near_part(0, 0, V)
     base(1)
     arrive(p_rows)
     for p in reversed(range(PX)):
         arrive(s_core[p], s_next[p])
         solve(p)
-    q_plane = to_right(Q.at[PX - 1], QH)
+    q_plane = to_right(Q.at[PX - 1], QH, True)
     start(q_plane)
     c_out = pltpu.make_async_copy(CO, cor, out_sem.at[3])
     c_out.start()
-    f_halo = {}
     sweep(1)
-    f_halo[1], f_pass = by_planes(1, 1, FS)
+    across_middle, f_pass[1], _ = middle(1, 1, FS, (2, 2, 2))
+    f_halo[1] = both_ways(1, 1, FS) + across_middle
     edge[1, 1] = edges(1, 1, FS)
+    v_pass[0](0, 1, 2)
     pl.when(at_middle)(lambda: send_corner[0, 2](v_halo[2]))
-    v0_later()
-    arrive_z(0, 2)
     base(2)
     sweep(2)
-    f_halo[2] = both_ways(1, 2, FS)
-    start(f_halo[2][0])
-    start(f_halo[2][1])
+    across_middle, f_pass[2], _ = middle(1, 2, FS, (2, 2, 2))
+    f_halo[2] = both_ways(1, 2, FS) + across_middle
     edge[1, 2] = edges(1, 2, FS)
     send_corner[0, 0](v_halo[0])
-    f_pass(0)
-    arrive_z(0, 0)
+    near_part(1, 1, FS)
     base(0)
     arrive(q_plane)
     sweep(0)
-    f_ends = both_ways(1, 0, FS, rows=pl.ds(0, 8)) + both_ways(1, 0, FS, rows=pl.ds(24, 8))
-    f_rest = both_ways(1, 0, FS, rows=pl.ds(8, 16))
-    for copy in f_ends + f_rest:
-        start(copy)
+    f_ends = sum((both_ways(1, 0, FS, rows=pl.ds(at, 8), direct=True) for at in (0, 24)), ())
+    f_rest = both_ways(1, 0, FS, rows=pl.ds(8, 16), direct=True)
     edge[1, 0] = edges(1, 0, FS)
-    f_pass(1)
-    f_pass(2)
+    f_pass[1](0, 1, 2)
+    near_part(1, 2, FS)
 
     outs = []
 
     def finish(c):
-        OB[c] = FS[c] * (2.0 - RE[...] * H[...]) - H[...] * operate(1, c, FS)
+        OB[c] = FS[c] * (2.0 - RE[...] * H[...]) - H[...] * operate(1, c)
         copy = pltpu.make_async_copy(OB.at[c], out.at[c], out_sem.at[c])
         copy.start()
         outs.append(copy)
 
     send_corner[1, 1](f_halo[1])
-    arrive_z(1, 1)
+    f_pass[2](0, 1, 2)
+    near_part(1, 0, FS)
     finish(1)
     send_corner[1, 2](f_halo[2])
     send_corner[1, 0](f_ends)
-    arrive_z(1, 2)
     finish(2)
     for copy in f_rest:
         arrive(copy)
-    arrive_z(1, 0)
     finish(0)
 
     for copy, sends in started:
@@ -468,13 +504,14 @@
     halo = (2, 3, 3, PZ, NY)
     scratch = [
         f32(3, *grid), f32(*grid), f32(3, *grid), f32(*grid), f32(*grid), f32(PX, NY), f32(40, 128),
-        b16(2 * ROWS, DEPTH), b16(2 * ROWS, DEPTH), b16(NY, NY), b16(NY, NY), b16(NY, NY),
+        b16(2 * ROWS, 256 + FAR), b16(2 * ROWS, 256 + FAR), b16(2, 256, 256), b16(2, 256, 256), b16(2, 256, 256),
         f32(*halo), f32(*halo), f32(2, 3, EDGE, NY), f32(2, 3, EDGE, NY),
         f32(PX, 4 * PZ, NY), f32(PZ, NY), f32(8, NY), f32(8, NY),
         f32(*grid), f32(*grid), f32(*grid), f32(3, *grid), f32(3, *grid), f32(3, *grid),
-        b16(DEPTH, NY), b16(DEPTH, NY), f32(2, 3, PZ, NY), f32(8, NY),
+        b16(NEAR, NY), b16(NEAR, NY), b16(FAR, NY), b16(FAR, NY),
+        f32(3, 2 * ROWS, NY), f32(*halo), f32(8, NY),
         pltpu.SemaphoreType.DMA((16,)), pltpu.SemaphoreType.DMA((4,)),
-        pltpu.SemaphoreType.DMA((128,)), pltpu.SemaphoreType.DMA((128,)),
+        pltpu.SemaphoreType.DMA((144,)), pltpu.SemaphoreType.DMA((144,)),
     ]
     return pl.pallas_call(
         functools.partial(kernel, count_x),

time: 59.4 us -> 55.7 us (0.938)
  the two profiles are of different devices: /device:TPU:1 before, /device:TPU:9 now
where the time goes in v3:
time: 55.7 us; the launch traced here: 55.6 us
  Pallas kernels  52.2 us (94%)
  local copies, waits for them, and re-layouts  2.81 us (5%)
  between operations  0.65 us (1%)
    pallas_call x1, Pallas kernels, shards(): pl.pallas_call(functools.partial(kernel, count_x), name='stokes', out_sha...  52.2 us
    unnamed x4, local copies, waits for them, and re-layouts  2.81 us

profile of v3, /device:TPU:9, one launch (start us, length us, event | category | flops | bytes accessed | tf_op | source)
XLA Modules:
  0.0 55.6 jit_solution(18000905532328283298)
XLA Ops:
  0.6 52.2 %stokes.1 = (f32[3,4,32,512]{3,2,1,0:T(8,128)}, f32[4,32,512]{2,1,0:T(8,128)}) custom-call(f32[3,4,32,512]{3,2,1,0:T(8,128)} %vel.1, f32[4,32,512]{2,1,0:T(8,128)} %prs.1, f32[3,4,32,512]{3,2,1,0:T(8,128)} %mom.1, f32[4,32,512]{2,1,0:T(8,128)} %con.1, f32[4,32,512]{2,1,0:T(8,128)} %rea.1, f32[4,512]{1,0:T(4,128)} %pwt.1, f32[128,128]{1,0:T(8,128)} %mzi.1, ...), custom_call_target="tpu_custom_call" | custom-call | tf_op jit(solution)/shard_map/stokes/pallas_call | solution.py:516
  52.8 0.0 copy-start
  52.8 2.1 %copy.16 = f32[3,4,32,512]{3,2,1,0:T(8,128)} copy(f32[3,4,32,512]{3,2,1,0:T(8,128)} %get-tuple-element.4) | data formatting | bytes 1572864
  54.9 0.0 copy-done
  54.9 0.7 %copy.17 = f32[4,32,512]{2,1,0:T(8,128)} copy(f32[4,32,512]{2,1,0:T(8,128)S(1)} %copy-done) | data formatting | bytes 524288
Async XLA Ops:
  52.8 2.1 %copy-start = (f32[4,32,512]{2,1,0:T(8,128)S(1)}, f32[4,32,512]{2,1,0:T(8,128)}, u32[]{:S(2)}) copy-start(f32[4,32,512]{2,1,0:T(8,128)} %get-tuple-element.5) | copy-start | bytes 786436
